TPU v7x, 512 devices: a whole 4x4x16 slice. The times are simulated.
512 devices in a mesh: wide: 64 (over z, y), ply: 8 (over x, core).
Axes of the slice: x: 4, y: 4, z: 16, core: 2. Of those that a mesh axis runs over, the one named last changes fastest.
Arguments:
- interior_inverse: bfloat16 [1536, 640, 640], P(('wide', 'ply')), may hold values from -0.25 to 0.25
- coupling: bfloat16 [1536, 640, 512], P(('wide', 'ply')), may hold values from -0.83984375 to 0.83984375
- boundary_stiffness: bfloat16 [1536, 512], P(('wide', 'ply')), may hold values from 1 to 10
- interior_load: bfloat16 [1536, 640], P(('wide', 'ply')), may hold values from -6 to 6
- boundary_load: bfloat16 [1536, 512], P(('wide', 'ply')), may hold values from -6 to 6
- touch_ply: int32 [6144, 1], P(('wide', 'ply')), may hold values from 0 to 7; in each aligned block of 12 rows (0 to 11, 12 to 23, ...) at most 3 rows name the same one
- touch_slot: int32 [6144], P(('wide', 'ply')), may hold values from 0 to 3
- source_position: int32 [8, 256], P('ply'), may hold values from 0 to 255, each once within a row
Outputs:
- interface_blocks: float32 [8, 128, 256, 128], P('ply', 'wide')
- interface_loads: float32 [8, 128, 256], P('ply', 'wide')
Inputs may be any that keep to these rules, and one draw needn't show every extreme that they name: `touch_ply`: among the items of one device, at most 3 have the same ply index, and some device reaches 3. `source_position`: each row holds every owner position once.
All inputs are finite; a program needn't handle non-finite values.
Results may differ from a plain program's by a relative error of at most 0.004.
Values may be sent and summed in bfloat16 or wider, within the bound.
No kernel may reach another device: no remote copies, remote signals or barrier semaphores. Data moves between devices by JAX's collectives and lax.ppermute only.
A program may use at most 64 MiB of HBM per device.

v0:
```python
import jax
import jax.numpy as jnp
from jax import lax
from jax.sharding import PartitionSpec as P

PR = 128
NPS = 4
P_OWN = 4


def on_device(
    interior_inverse,
    coupling,
    boundary_stiffness,
    interior_load,
    boundary_load,
    touch_ply,
    touch_slot,
    source_position,
):
    wide_count = lax.axis_size("wide")
    ply_count = lax.axis_size("ply")
    sub_count = interior_inverse.shape[0]
    inner_size = interior_inverse.shape[1]
    item_count = sub_count * NPS
    capacity = (item_count + ply_count - 1) // ply_count + 1
    slot_count = ply_count * capacity
    inner_solve = jnp.einsum(
        "smn,snb->smb", interior_inverse, coupling, preferred_element_type=jnp.float32
    ).astype(jnp.bfloat16)
    solved = jnp.einsum(
        "smn,sn->sm", interior_inverse, interior_load, preferred_element_type=jnp.float32
    ).astype(jnp.bfloat16)
    split_coupling = coupling.reshape(sub_count, inner_size, NPS, PR)
    split_inner = inner_solve.reshape(sub_count, inner_size, NPS, PR)
    product = jnp.einsum(
        "smka,smkc->skac", split_coupling, split_inner, preferred_element_type=jnp.float32
    )
    identity = jnp.eye(PR, dtype=jnp.float32)
    stiffness = boundary_stiffness.astype(jnp.float32).reshape(sub_count, NPS, PR)
    panels = (
        (stiffness[..., None] * identity - product).astype(jnp.bfloat16).reshape(item_count, PR, PR)
    )
    carried = jnp.einsum("sm,smb->sb", solved, coupling, preferred_element_type=jnp.float32)
    condensed = (
        (boundary_load.astype(jnp.float32) - carried).astype(jnp.bfloat16).reshape(item_count, PR)
    )
    dest_ply = touch_ply[:, 0]
    item_order = jnp.arange(item_count, dtype=jnp.int32)
    earlier = (dest_ply[:, None] == dest_ply[None, :]) & (item_order[None, :] < item_order[:, None])
    bucket_rank = jnp.sum(earlier.astype(jnp.int32), axis=1)
    position = dest_ply * capacity + bucket_rank
    placed = position[None, :] == jnp.arange(slot_count, dtype=jnp.int32)[:, None]
    place_matrix = placed.astype(jnp.bfloat16)
    slot_ids = jnp.max(jnp.where(placed, touch_slot[None, :], -1), axis=1)
    target = source_position[0]
    row_share = PR // wide_count
    split_panels = panels.reshape(item_count, wide_count, row_share, PR)
    send_panels = jnp.einsum(
        "pi,iwrc->wprc", place_matrix, split_panels, preferred_element_type=jnp.float32
    )
    send_panels = send_panels.astype(jnp.bfloat16).reshape(
        wide_count, ply_count, capacity, row_share, PR
    )
    split_loads = condensed.reshape(item_count, wide_count, row_share)
    send_loads = jnp.einsum(
        "pi,iwr->wpr", place_matrix, split_loads, preferred_element_type=jnp.float32
    )
    send_loads = send_loads.astype(jnp.bfloat16).reshape(wide_count, ply_count, capacity, row_share)
    send_slots = jnp.broadcast_to(
        slot_ids.reshape(1, ply_count, capacity), (wide_count, ply_count, capacity)
    )
    got_panels, got_loads, got_slots = (
        lax.all_to_all(
            lax.all_to_all(send_panels, "wide", split_axis=0, concat_axis=0, tiled=True),
            "ply",
            split_axis=1,
            concat_axis=1,
            tiled=True,
        ),
        lax.all_to_all(
            lax.all_to_all(send_loads, "wide", split_axis=0, concat_axis=0, tiled=True),
            "ply",
            split_axis=1,
            concat_axis=1,
            tiled=True,
        ),
        lax.all_to_all(
            lax.all_to_all(send_slots, "wide", split_axis=0, concat_axis=0, tiled=True),
            "ply",
            split_axis=1,
            concat_axis=1,
            tiled=True,
        ),
    )
    source_wide = jnp.arange(wide_count, dtype=jnp.int32)[:, None, None]
    item_keys = jnp.where(got_slots >= 0, source_wide * P_OWN + got_slots, -1).reshape(-1)
    owner_marks = (item_keys[None, :] == target[:, None]).astype(jnp.bfloat16)
    out_blocks = jnp.einsum(
        "gi,irc->rgc",
        owner_marks,
        got_panels.reshape(-1, row_share, PR),
        preferred_element_type=jnp.float32,
    )
    out_loads = jnp.einsum(
        "gi,ir->rg",
        owner_marks,
        got_loads.reshape(-1, row_share),
        preferred_element_type=jnp.float32,
    )
    return (out_blocks[None], out_loads[None])


def solution(mesh):
    return jax.shard_map(
        on_device,
        mesh=mesh,
        in_specs=(
            P(("wide", "ply"), None, None),
            P(("wide", "ply"), None, None),
            P(("wide", "ply"), None),
            P(("wide", "ply"), None),
            P(("wide", "ply"), None),
            P(("wide", "ply"), None),
            P(("wide", "ply")),
            P("ply", None),
        ),
        out_specs=(P("ply", "wide", None, None), P("ply", "wide", None)),
        check_vma=False,
    )
```

profile of v0, /device:TPU:1, one launch (start us, length us, event | category | flops | bytes accessed | tf_op | source)
XLA Modules:
  0.0 152.5 jit_solution(17736245974687730358)
XLA Ops:
  0.6 1.0 convert_reduce_fusion
  1.6 0.7 multiply_add_fusion
  2.3 0.7 select_reduce_fusion
  3.1 0.1 broadcast_in_dim.38
  3.1 0.1 copy.69
  3.2 0.7 broadcast_in_dim.39
  3.9 19.3 %all-to-all-start.2 = ((s32[64,8,3]{1,2,0:T(4,128)}), s32[64,8,3]{1,2,0:T(4,128)S(1)}, u32[]{:S(2)}, u32[]{:S(2)}) async-start(s32[64,8,3]{1,2,0:T(4,128)} %broadcast_in_dim.39), calls=%async_computation.2 | async-start | bytes 262144 | tf_op jit(solution)/shard_map/all_to_all | solution.py:89
  23.2 4.8 %convolution_convert_fusion = bf16[3,640,512]{1,2,0:T(8,128)(2,1)} fusion(bf16[3,640,640]{2,1,0:T(8,128)(2,1)S(1)} %copy-done, bf16[3,640,512]{2,1,0:T(8,128)(2,1)} %param.9), kind=kOutput, calls=%fused_computation.3 | convolution fusion | flops 1259274240 | bytes 6389760 | tf_op jit(solution)/shard_map/smn,snb->smb/dot_general | solution.py:28
  28.0 0.8 fusion.26
  28.8 0.8 copy-done.1
  29.6 0.4 fusion.24
  29.9 0.4 reshape_reshape.7
  30.4 0.2 copy.73
  30.5 0.3 fusion.7
  30.8 4.0 %copy.86 = bf16[3,640,512]{1,2,0:T(8,128)(2,1)} copy(bf16[3,640,512]{2,1,0:T(8,128)(2,1)} %param.9) | data formatting | bytes 3932160 | tf_op jit(solution)/shard_map/reshape | solution.py:34
  34.9 0.8 copy.75
  35.6 2.5 %all-to-all-done.2 = s32[64,8,3]{1,2,0:T(4,128)S(1)} async-done(((s32[64,8,3]{1,2,0:T(4,128)}), s32[64,8,3]{1,2,0:T(4,128)S(1)}, u32[]{:S(2)}, u32[]{:S(2)}) %all-to-all-start.2) | async-done | bytes 6176 | tf_op jit(solution)/shard_map/all_to_all | solution.py:89
  38.1 12.0 %all-to-all-start.4 = ((bf16[64,8,3,2]{1,3,2,0:T(2,128)(2,1)}), bf16[64,8,3,2]{1,3,2,0:T(2,128)(2,1)S(1)}, u32[]{:S(2)}, u32[]{:S(2)}) async-start(bf16[64,8,3,2]{1,3,2,0:T(2,128)(2,1)} %copy.75), calls=%async_computation.4 | async-start | bytes 196608 | tf_op jit(solution)/shard_map/all_to_all | solution.py:82
  50.1 3.0 %fusion.5 = bf16[3,4,128,128]{3,2,1,0:T(8,128)(2,1)S(1)} fusion(bf16[3,640,4,128]{1,3,2,0:T(8,128)(2,1)} %bitcast.81, bf16[3,640,4,128]{1,3,2,0:T(8,128)(2,1)} %bitcast.69, f32[128,128]{1,0:T(8,128)S(1)} %fusion.17, f32[3,4,128]{2,1,0:T(4,128)S(1)} %reshape.56), kind=kOutput, calls=%fused_computation.9 | convolution fusion | flops 252248064 | bytes 4397056 | tf_op jit(solution)/shard_map/smka,smkc->skac/dot_general | solution.py:36
  53.1 0.1 copy.70
  53.2 0.7 reshape.64
  53.9 10.7 %all-to-all-done.4 = bf16[64,8,3,2]{1,3,2,0:T(2,128)(2,1)S(1)} async-done(((bf16[64,8,3,2]{1,3,2,0:T(2,128)(2,1)}), bf16[64,8,3,2]{1,3,2,0:T(2,128)(2,1)S(1)}, u32[]{:S(2)}, u32[]{:S(2)}) %all-to-all-start.4) | async-done | bytes 6176 | tf_op jit(solution)/shard_map/all_to_all | solution.py:82
  64.7 7.2 %all-to-all-start.3 = ((s32[8,1,192]{2,1,0:T(1,128)}), s32[8,1,192]{2,1,0:T(1,128)S(1)}, u32[]{:S(2)}, u32[]{:S(2)}) async-start(s32[8,1,192]{2,1,0:T(1,128)} %reshape.64), calls=%async_computation.3 | async-start | bytes 16384 | tf_op jit(solution)/shard_map/all_to_all | solution.py:88
  71.9 0.5 fusion.3
  72.4 0.2 copy.65
  72.6 1.7 %copy.66 = bf16[64,8,3,2,128]{4,3,2,1,0:T(2,128)(2,1)} copy(bf16[64,8,3,2,128]{4,0,3,2,1:T(8,128)(2,1)S(1)} %bitcast.68) | data formatting | bytes 1572864 | tf_op jit(solution)/shard_map/reshape | solution.py:62
  74.3 2.2 %all-to-all-done.3 = s32[8,1,192]{2,1,0:T(1,128)S(1)} async-done(((s32[8,1,192]{2,1,0:T(1,128)}), s32[8,1,192]{2,1,0:T(1,128)S(1)}, u32[]{:S(2)}, u32[]{:S(2)}) %all-to-all-start.3) | async-done | bytes 6176 | tf_op jit(solution)/shard_map/all_to_all | solution.py:88
  76.5 4.6 %all-to-all-start = ((bf16[64,8,3,2,128]{4,3,2,1,0:T(2,128)(2,1)}), bf16[64,8,3,2,128]{4,3,2,1,0:T(2,128)(2,1)S(1)}, u32[]{:S(2)}, u32[]{:S(2)}) async-start(bf16[64,8,3,2,128]{4,3,2,1,0:T(2,128)(2,1)} %copy.66), calls=%async_computation | async-start | bytes 1572864 | tf_op jit(solution)/shard_map/all_to_all | solution.py:75
  81.1 0.1 copy.76
  81.2 0.7 reshape.66
  81.9 40.3 %all-to-all-done = bf16[64,8,3,2,128]{4,3,2,1,0:T(2,128)(2,1)S(1)} async-done(((bf16[64,8,3,2,128]{4,3,2,1,0:T(2,128)(2,1)}), bf16[64,8,3,2,128]{4,3,2,1,0:T(2,128)(2,1)S(1)}, u32[]{:S(2)}, u32[]{:S(2)}) %all-to-all-start) | async-done | bytes 786464 | tf_op jit(solution)/shard_map/all_to_all | solution.py:75
  122.3 7.1 %all-to-all-start.5 = ((bf16[8,2,192]{2,1,0:T(2,128)(2,1)}), bf16[8,2,192]{2,1,0:T(2,128)(2,1)S(1)}, u32[]{:S(2)}, u32[]{:S(2)}) async-start(bf16[8,2,192]{2,1,0:T(2,128)(2,1)} %reshape.66), calls=%async_computation.5 | async-start | bytes 16384 | tf_op jit(solution)/shard_map/all_to_all | solution.py:81
  129.4 1.5 copy.67
  130.9 3.1 %all-to-all-done.5 = bf16[8,2,192]{2,1,0:T(2,128)(2,1)S(1)} async-done(((bf16[8,2,192]{2,1,0:T(2,128)(2,1)}), bf16[8,2,192]{2,1,0:T(2,128)(2,1)S(1)}, u32[]{:S(2)}, u32[]{:S(2)}) %all-to-all-start.5) | async-done | bytes 6176 | tf_op jit(solution)/shard_map/all_to_all | solution.py:81
  134.0 4.1 %all-to-all-start.1 = ((bf16[64,8,3,2,128]{4,3,2,0,1:T(2,128)(2,1)}), bf16[64,8,3,2,128]{4,3,2,0,1:T(2,128)(2,1)S(1)}, u32[]{:S(2)}, u32[]{:S(2)}) async-start(bf16[64,8,3,2,128]{4,3,2,0,1:T(2,128)(2,1)} %copy.67), calls=%async_computation.1 | async-start | bytes 1572864 | tf_op jit(solution)/shard_map/all_to_all | solution.py:74
  138.2 0.5 broadcast.15
  138.7 0.7 reduce
  139.4 0.1 reshape.65
  139.4 0.2 copy.71
  139.6 0.2 eq.57
  139.8 0.1 reshape.67
  139.9 0.2 copy.77
  140.2 0.4 reshape.55
  140.5 1.0 fusion.8
  141.5 8.9 %all-to-all-done.1 = bf16[64,8,3,2,128]{4,3,2,0,1:T(2,128)(2,1)S(1)} async-done(((bf16[64,8,3,2,128]{4,3,2,0,1:T(2,128)(2,1)}), bf16[64,8,3,2,128]{4,3,2,0,1:T(2,128)(2,1)S(1)}, u32[]{:S(2)}, u32[]{:S(2)}) %all-to-all-start.1) | async-done | bytes 786464 | tf_op jit(solution)/shard_map/all_to_all | solution.py:74
  150.5 0.5 copy.68
  151.0 0.6 fusion.6
  151.6 0.8 copy.78
  (18 shorter events, 0.1 us)
Async XLA Ops:
  0.6 22.6 %copy-start = (bf16[3,640,640]{2,1,0:T(8,128)(2,1)S(1)}, bf16[3,640,640]{2,1,0:T(8,128)(2,1)}, u32[]{:S(2)}) copy-start(bf16[3,640,640]{2,1,0:T(8,128)(2,1)} %param.8) | copy-start | bytes 7372804
  3.9 34.2 %all-to-all-start.2 = ((s32[64,8,3]{1,2,0:T(4,128)}), s32[64,8,3]{1,2,0:T(4,128)S(1)}, u32[]{:S(2)}, u32[]{:S(2)}) async-start(s32[64,8,3]{1,2,0:T(4,128)} %broadcast_in_dim.39), calls=%async_computation.2 | async-start | bytes 262144 | tf_op jit(solution)/shard_map/all_to_all | solution.py:89
  23.2 4.8 %copy-start.2 = (bf16[3,640]{1,0:T(4,128)(2,1)S(1)}, bf16[3,640]{1,0:T(4,128)(2,1)}, u32[]{:S(2)}) copy-start(bf16[3,640]{1,0:T(4,128)(2,1)} %param.11) | copy-start | bytes 11524
  28.0 1.5 %copy-start.1 = (bf16[3,640,512]{2,1,0:T(8,128)(2,1)S(1)}, bf16[3,640,512]{2,1,0:T(8,128)(2,1)}, u32[]{:S(2)}) copy-start(bf16[3,640,512]{2,1,0:T(8,128)(2,1)} %param.9) | copy-start | bytes 5898244
  28.0 1.9 %copy-start.3 = (bf16[3,512]{1,0:T(4,128)(2,1)S(1)}, bf16[3,512]{1,0:T(4,128)(2,1)}, u32[]{:S(2)}) copy-start(bf16[3,512]{1,0:T(4,128)(2,1)} %param.12) | copy-start | bytes 9220
  30.8 4.0 %copy-start.4 = (bf16[3,512]{1,0:T(4,128)(2,1)S(1)}, bf16[3,512]{1,0:T(4,128)(2,1)}, u32[]{:S(2)}) copy-start(bf16[3,512]{1,0:T(4,128)(2,1)} %param.10) | copy-start | bytes 9220
  38.1 26.6 %all-to-all-start.4 = ((bf16[64,8,3,2]{1,3,2,0:T(2,128)(2,1)}), bf16[64,8,3,2]{1,3,2,0:T(2,128)(2,1)S(1)}, u32[]{:S(2)}, u32[]{:S(2)}) async-start(bf16[64,8,3,2]{1,3,2,0:T(2,128)(2,1)} %copy.75), calls=%async_computation.4 | async-start | bytes 196608 | tf_op jit(solution)/shard_map/all_to_all | solution.py:82
  64.7 11.8 %all-to-all-start.3 = ((s32[8,1,192]{2,1,0:T(1,128)}), s32[8,1,192]{2,1,0:T(1,128)S(1)}, u32[]{:S(2)}, u32[]{:S(2)}) async-start(s32[8,1,192]{2,1,0:T(1,128)} %reshape.64), calls=%async_computation.3 | async-start | bytes 16384 | tf_op jit(solution)/shard_map/all_to_all | solution.py:88
  76.5 45.8 %all-to-all-start = ((bf16[64,8,3,2,128]{4,3,2,1,0:T(2,128)(2,1)}), bf16[64,8,3,2,128]{4,3,2,1,0:T(2,128)(2,1)S(1)}, u32[]{:S(2)}, u32[]{:S(2)}) async-start(bf16[64,8,3,2,128]{4,3,2,1,0:T(2,128)(2,1)} %copy.66), calls=%async_computation | async-start | bytes 1572864 | tf_op jit(solution)/shard_map/all_to_all | solution.py:75
  122.3 11.7 %all-to-all-start.5 = ((bf16[8,2,192]{2,1,0:T(2,128)(2,1)}), bf16[8,2,192]{2,1,0:T(2,128)(2,1)S(1)}, u32[]{:S(2)}, u32[]{:S(2)}) async-start(bf16[8,2,192]{2,1,0:T(2,128)(2,1)} %reshape.66), calls=%async_computation.5 | async-start | bytes 16384 | tf_op jit(solution)/shard_map/all_to_all | solution.py:81
  129.4 11.1 %copy-start.5 = (s32[1,256]{1,0:T(1,128)S(1)}, s32[1,256]{1,0:T(1,128)}, u32[]{:S(2)}) copy-start(s32[1,256]{1,0:T(1,128)} %param.15) | copy-start | bytes 3076
  134.0 16.5 %all-to-all-start.1 = ((bf16[64,8,3,2,128]{4,3,2,0,1:T(2,128)(2,1)}), bf16[64,8,3,2,128]{4,3,2,0,1:T(2,128)(2,1)S(1)}, u32[]{:S(2)}, u32[]{:S(2)}) async-start(bf16[64,8,3,2,128]{4,3,2,0,1:T(2,128)(2,1)} %copy.67), calls=%async_computation.1 | async-start | bytes 1572864 | tf_op jit(solution)/shard_map/all_to_all | solution.py:74
where the time goes:
time: 153 us; the launch traced here: 152 us
  waiting for transfers between devices  67.8 us (44%)
  starting transfers between devices  54.4 us (36%)
  local copies, waits for them, and re-layouts  15 us (10%)
  matrix products  11.3 us (7%)
  other arithmetic  3.12 us (2%)
    all_to_all x1, waiting for transfers between devices, on_device(): lax.all_to_all(send_panels, 'wide', split_axis=0, concat_axis=0, tiled=True)  40.3 us
    all_to_all x1, starting transfers between devices, on_device(): lax.all_to_all(send_slots, 'wide', split_axis=0, concat_axis=0, tiled=True)  19.3 us
    all_to_all x1, starting transfers between devices, on_device(): lax.all_to_all(send_loads, 'wide', split_axis=0, concat_axis=0, tiled=True)  12 us
    all_to_all x1, waiting for transfers between devices, on_device(): lax.all_to_all(send_loads, 'wide', split_axis=0, concat_axis=0, tiled=True)  10.7 us
    all_to_all x1, waiting for transfers between devices, on_device(): lax.all_to_all(lax.all_to_all(send_panels, 'wide', split_axis=0, concat_a...  8.95 us
    all_to_all x1, starting transfers between devices, on_device(): lax.all_to_all(lax.all_to_all(send_slots, 'wide', split_axis=0, concat_ax...  7.21 us
    all_to_all x1, starting transfers between devices, on_device(): lax.all_to_all(lax.all_to_all(send_loads, 'wide', split_axis=0, concat_ax...  7.11 us
    dot_general x1, matrix products, on_device(): jnp.einsum('smn,snb->smb', interior_inverse, coupling, preferred_element_...  4.81 us
  transfers between devices with their start and end apart: 6, of which 6 were waited for; matrix products, arithmetic and copies ran while one was open for 15% of the time, Pallas kernels for 0%

commit v1 on v0

v1 whole, which is shorter than its diff:
```python
import functools

import jax
import jax.numpy as jnp
from jax import lax
from jax.experimental import pallas as pl
from jax.experimental.pallas import tpu as pltpu
from jax.sharding import PartitionSpec as P

PR = 128
NPS = 4
P_OWN = 4
CAP = 3
N_Z = 16
N_Y = 4
BITS = 2
SHARE = N_Z * BITS
CHUNK = CAP * SHARE + 8
CODE_ROW = CAP
LOADS = SHARE * P_OWN
BACK = N_Y * P_OWN * BITS + 8
VMEM_LIMIT = 40 * 1024 * 1024


def iota(shape, axis):
    return lax.broadcasted_iota(jnp.int32, shape, axis)


def condense_kernel(
    ply_ref,
    slot_ref,
    inverse_hbm,
    coupling_hbm,
    stiffness_ref,
    interior_ref,
    boundary_ref,
    out_ref,
    inverse_buf,
    coupling_buf,
    extra,
    count,
    sems,
):
    subs, inner_size, width = coupling_buf.shape
    plies = extra.shape[0]
    copies = []
    for s in range(subs):
        pair = (
            pltpu.make_async_copy(inverse_hbm.at[s], inverse_buf.at[s], sems.at[0, s]),
            pltpu.make_async_copy(coupling_hbm.at[s], coupling_buf.at[s], sems.at[1, s]),
        )
        for copy in pair:
            copy.start()
        copies.append(pair)
    out_ref[...] = jnp.zeros_like(out_ref)
    extra[...] = jnp.where(iota(extra.shape, 1) == CODE_ROW, -1.0, 0.0)
    for q in range(plies):
        count[q] = 0
    lane = iota((1, PR), 1)
    row_code = (lane % N_Z) * (BITS * P_OWN) + ((lane // N_Z) % BITS) * P_OWN
    row_item = lane // SHARE
    same = iota((PR, PR), 0) == iota((PR, PR), 1)
    row = iota((PR, PR), 0)
    source = (row % N_Z) * (N_Y * BITS) + (row // SHARE) * BITS + (row // N_Z) % BITS
    order = (source == iota((PR, PR), 1)).astype(jnp.bfloat16)
    stiffness = stiffness_ref[...].astype(jnp.float32)
    interior = interior_ref[...].astype(jnp.float32)
    boundary = boundary_ref[...].astype(jnp.float32)
    for s in range(subs):
        for copy in copies[s]:
            copy.wait()
        inverse = inverse_buf[s]
        load = jnp.broadcast_to(interior[s : s + 1], (16, inner_size)).astype(jnp.bfloat16)
        solved = lax.dot_general(
            load, inverse, (((1,), (1,)), ((), ())), preferred_element_type=jnp.float32
        ).astype(jnp.bfloat16)
        carried = jnp.dot(solved, coupling_buf[s], preferred_element_type=jnp.float32)
        condensed = boundary[s : s + 1] - carried[0:1]
        condensed = condensed.astype(jnp.bfloat16).astype(jnp.float32)
        for pair in range(width // (2 * PR)):
            columns = coupling_buf[s, :, pair * 2 * PR : (pair + 1) * 2 * PR]
            inner = jnp.dot(inverse, columns, preferred_element_type=jnp.float32)
            inner = inner.astype(jnp.bfloat16)
            product = lax.dot_general(
                columns, inner, (((0,), (0,)), ((), ())), preferred_element_type=jnp.float32
            )
            for half in range(2):
                k = pair * 2 + half
                item = s * NPS + k
                block = product[half * PR : (half + 1) * PR, half * PR : (half + 1) * PR]
                diagonal = jnp.where(same, stiffness[s : s + 1, k * PR : (k + 1) * PR], 0.0)
                panel = (diagonal - block).astype(jnp.bfloat16)
                panel = jnp.dot(order, panel, preferred_element_type=jnp.float32)
                panel = panel.astype(jnp.bfloat16)
                q = ply_ref[item, 0]
                slot = slot_ref[item]
                rank = count[q]
                count[q] = rank + 1
                for y in range(N_Y):
                    out_ref[y * plies + q, pl.ds(pl.multiple_of(rank * SHARE, SHARE), SHARE), :] = (
                        panel[y * SHARE : (y + 1) * SHARE]
                    )
                extra[q, pl.ds(rank, 1), :] = condensed[:, k * PR : (k + 1) * PR]
                codes = extra[q, CODE_ROW : CODE_ROW + 1, :]
                codes = jnp.where(row_item == rank, (row_code + slot).astype(jnp.float32), codes)
                codes = jnp.where(
                    lane == CAP * SHARE + rank, (LOADS + slot).astype(jnp.float32), codes
                )
                extra[q, CODE_ROW : CODE_ROW + 1, :] = codes
    is_code = iota((8, PR), 0) == CODE_ROW
    for q in range(plies):
        rows = extra[q]
        for y in range(N_Y):
            turned = rows if y == 0 else pltpu.roll(rows, PR - BITS * y, 1)
            out_ref[y * plies + q, CAP * SHARE : CHUNK, :] = jnp.where(
                is_code, rows, turned
            ).astype(jnp.bfloat16)


def combine_kernel(got_ref, out_ref):
    plies = got_ref.shape[0] // N_Y
    sum_rows = iota((LOADS + 8, CHUNK), 0).astype(jnp.float32)
    sums = []
    for y in range(N_Y):
        total = jnp.zeros((LOADS + 8, PR), jnp.float32)
        for q in range(plies):
            message = got_ref[y * plies + q]
            tail = message[CAP * SHARE : CHUNK].astype(jnp.float32)
            codes = tail[CODE_ROW : CODE_ROW + 1, 0:CHUNK]
            choose = (sum_rows == codes).astype(jnp.bfloat16)
            total = total + jnp.dot(choose, message, preferred_element_type=jnp.float32)
        sums.append(total)
    loads = jnp.concatenate([t[LOADS : LOADS + P_OWN] for t in sums], axis=0)
    loads = jnp.concatenate([loads, jnp.zeros((PR - N_Y * P_OWN, PR), jnp.float32)], axis=0)
    loads = loads.T
    step = BITS * P_OWN
    for z in range(N_Z):
        rows = [t[z * step : (z + 1) * step] for t in sums] + [loads[z * step : (z + 1) * step]]
        out_ref[z] = jnp.concatenate(rows, axis=0).astype(jnp.bfloat16)


def place_kernel(target_ref, got_ref, blocks_ref, loads_ref):
    patches = target_ref.shape[1]
    target = target_ref[...]
    rows = N_Y * P_OWN * BITS
    slots = P_OWN - 1
    blocks = got_ref[:, 0:rows, :].reshape(N_Z * rows, PR)
    loads = got_ref[:, rows:BACK, :].astype(jnp.float32).reshape(N_Z * 8, PR)
    loads = loads.astype(jnp.bfloat16)
    for bit in range(BITS):
        wanted = (target - (target & slots)) * BITS + bit * P_OWN + (target & slots)
        choose = (iota((N_Z * rows, patches), 0) == wanted).astype(jnp.bfloat16)
        blocks_ref[0, bit] = lax.dot_general(
            choose, blocks, (((0,), (0,)), ((), ())), preferred_element_type=jnp.float32
        )
        wanted = (target // (N_Y * P_OWN)) * 8 + bit
        choose = (iota((N_Z * 8, patches), 0) == wanted).astype(jnp.bfloat16)
        picked = lax.dot_general(
            loads, choose, (((0,), (0,)), ((), ())), preferred_element_type=jnp.float32
        )[0 : N_Y * P_OWN]
        mine = iota(picked.shape, 0) == target % (N_Y * P_OWN)
        loads_ref[0, bit : bit + 1, :] = jnp.sum(
            jnp.where(mine, picked, 0.0), axis=0, keepdims=True
        )


def vmem():
    return pl.BlockSpec(memory_space=pltpu.VMEM)


def smem():
    return pl.BlockSpec(memory_space=pltpu.SMEM)


def hbm():
    return pl.BlockSpec(memory_space=pl.ANY)


def on_device(
    interior_inverse,
    coupling,
    boundary_stiffness,
    interior_load,
    boundary_load,
    touch_ply,
    touch_slot,
    source_position,
):
    wide_count = lax.axis_size("wide")
    ply_count = lax.axis_size("ply")
    subs, inner_size, width = coupling.shape
    patches = source_position.shape[1]
    params = pltpu.CompilerParams(vmem_limit_bytes=VMEM_LIMIT)
    send = pl.pallas_call(
        condense_kernel,
        out_shape=jax.ShapeDtypeStruct((N_Y * ply_count, CHUNK, PR), jnp.bfloat16),
        in_specs=[smem(), smem(), hbm(), hbm(), vmem(), vmem(), vmem()],
        out_specs=vmem(),
        scratch_shapes=[
            pltpu.VMEM((subs, inner_size, inner_size), jnp.bfloat16),
            pltpu.VMEM((subs, inner_size, width), jnp.bfloat16),
            pltpu.VMEM((ply_count, 8, PR), jnp.float32),
            pltpu.SMEM((ply_count,), jnp.int32),
            pltpu.SemaphoreType.DMA((2, subs)),
        ],
        compiler_params=params,
        name="condense",
    )(
        touch_ply,
        touch_slot,
        interior_inverse,
        coupling,
        boundary_stiffness,
        interior_load,
        boundary_load,
    )
    plane = N_Y * ply_count
    got = lax.all_to_all(
        send,
        ("wide", "ply"),
        split_axis=0,
        concat_axis=0,
        tiled=True,
        axis_index_groups=[[z * plane + i for i in range(plane)] for z in range(N_Z)],
    )
    back = pl.pallas_call(
        combine_kernel,
        out_shape=jax.ShapeDtypeStruct((N_Z, BACK, PR), jnp.bfloat16),
        in_specs=[vmem()],
        out_specs=vmem(),
        compiler_params=params,
        name="combine",
    )(got)
    got = lax.all_to_all(
        back,
        "wide",
        split_axis=0,
        concat_axis=0,
        tiled=True,
        axis_index_groups=[[z * N_Y + y for z in range(N_Z)] for y in range(N_Y)],
    )
    return pl.pallas_call(
        place_kernel,
        out_shape=(
            jax.ShapeDtypeStruct((1, BITS, patches, PR), jnp.float32),
            jax.ShapeDtypeStruct((1, BITS, patches), jnp.float32),
        ),
        in_specs=[vmem(), vmem()],
        out_specs=(vmem(), vmem()),
        compiler_params=params,
        name="place",
    )(source_position, got)


def solution(mesh):
    return jax.shard_map(
        on_device,
        mesh=mesh,
        in_specs=(
            P(("wide", "ply"), None, None),
            P(("wide", "ply"), None, None),
            P(("wide", "ply"), None),
            P(("wide", "ply"), None),
            P(("wide", "ply"), None),
            P(("wide", "ply"), None),
            P(("wide", "ply")),
            P("ply", None),
        ),
        out_specs=(P("ply", "wide", None, None), P("ply", "wide", None)),
        check_vma=False,
    )
```

time: 153 us -> 70.5 us (0.46)
  the two profiles are of different devices: /device:TPU:1 before, /device:TPU:32 now
where the time goes in v1:
time: 70.5 us; the launch traced here: 70.1 us
  blocking collectives  52.4 us (74%)
  Pallas kernels  10.4 us (15%)
  local copies, waits for them, and re-layouts  6.7 us (10%)
    all_to_all x1, blocking collectives, on_device(): lax.all_to_all(back, 'wide', split_axis=0, concat_axis=0, tiled=True, axi...  30.1 us
    all_to_all x1, blocking collectives, on_device(): lax.all_to_all(send, ('wide', 'ply'), split_axis=0, concat_axis=0, tiled=...  22.3 us
    pallas_call x1, Pallas kernels, on_device(): pl.pallas_call(condense_kernel, out_shape=jax.ShapeDtypeStruct((N_Y * ply...  8.43 us
    unnamed x15, local copies, waits for them, and re-layouts  6.7 us

profile of v1, /device:TPU:32, one launch (start us, length us, event | category | flops | bytes accessed | tf_op | source)
XLA Modules:
  0.0 70.1 jit_solution(16957008507987371035)
XLA Ops:
  0.6 0.7 %copy.10.ply_ref = s32[12,1]{1,0:T(8,128)S(1)} copy(s32[12,1]{0,1:T(1,128)} %param.13) | data formatting | bytes 96 | tf_op args[5]
  1.4 0.0 copy-start
  1.4 1.7 %copy-done = bf16[3,640,640]{2,1,0:T(8,128)(2,1)S(1)} copy-done((bf16[3,640,640]{2,1,0:T(8,128)(2,1)S(1)}, bf16[3,640,640]{2,1,0:T(8,128)(2,1)}, u32[]{:S(2)}) %copy-start) | copy-done | bytes 2457624
  3.1 0.0 copy-start.1
  3.1 1.5 %copy-done.1 = bf16[3,640,512]{2,1,0:T(8,128)(2,1)S(1)} copy-done((bf16[3,640,512]{2,1,0:T(8,128)(2,1)S(1)}, bf16[3,640,512]{2,1,0:T(8,128)(2,1)}, u32[]{:S(2)}) %copy-start.1) | copy-done | bytes 1966104
  4.6 0.0 copy-start.2
  4.6 0.7 copy-done.2
  5.3 0.0 copy-start.3
  5.3 0.7 copy-done.3
  6.0 0.0 copy-start.4
  6.0 0.7 copy-done.4
  6.7 0.0 copy-start.6
  6.7 0.7 copy-done.6
  7.3 8.4 %condense.1 = bf16[32,104,128]{2,1,0:T(8,128)(2,1)S(1)} custom-call(s32[12,1]{1,0:T(8,128)S(1)} %copy.10.ply_ref, s32[12]{0:T(128)S(1)} %copy-done.6, bf16[3,640,640]{2,1,0:T(8,128)(2,1)S(1)} %copy-done, bf16[3,640,512]{2,1,0:T(8,128)(2,1)S(1)} %copy-done.1, bf16[3,512]{1,0:T(4,128)(2,1)S(1)} %copy-done.3, bf16[3,640]{1,0:T(4,128)(2,1)S(1)} %copy-done.2, ...), custom_call_target="tpu_custom_call" | custom-call | tf_op jit(solution)/shard_map/condense/pallas_call | solution.py:194
  15.8 0.0 copy-start.5
  15.8 22.3 %all_to_all.10.got_ref = bf16[32,104,128]{2,1,0:T(8,128)(2,1)S(1)} all-to-all(bf16[32,104,128]{2,1,0:T(8,128)(2,1)S(1)} %condense.1), channel_id=1, replica_groups={{0,1,2,3,4,5,6,7,8,9,10,11,12,13,14,15,16,17,18,19,20,21,22,23,24,25,26..., dimensions={0} | all-to-all | bytes 1703936 | tf_op jit(solution)/shard_map/all_to_all | solution.py:218
  38.1 0.8 %combine.1 = bf16[16,40,128]{2,1,0:T(8,128)(2,1)S(1)} custom-call(bf16[32,104,128]{2,1,0:T(8,128)(2,1)S(1)} %all_to_all.10.got_ref), custom_call_target="tpu_custom_call" | custom-call | tf_op jit(solution)/shard_map/combine/pallas_call | solution.py:226
  39.0 30.1 %all_to_all.11.got_ref = bf16[16,40,128]{2,1,0:T(8,128)(2,1)S(1)} all-to-all(bf16[16,40,128]{2,1,0:T(8,128)(2,1)S(1)} %combine.1), channel_id=1, replica_groups={{0,32,64,96,128,160,192,224,256,288,320,352,384,416,448,480},{8,40,72,1..., dimensions={0} | all-to-all | bytes 327680 | tf_op jit(solution)/shard_map/all_to_all | solution.py:234
  69.0 0.0 copy-done.5
  69.0 1.1 %place.1 = (f32[1,2,256,128]{3,2,1,0:T(8,128)}, f32[1,2,256]{2,1,0:T(2,128)}) custom-call(s32[1,256]{1,0:T(1,128)S(1)} %copy-done.5, bf16[16,40,128]{2,1,0:T(8,128)(2,1)S(1)} %all_to_all.11.got_ref), custom_call_target="tpu_custom_call" | custom-call | tf_op jit(solution)/shard_map/place/pallas_call | solution.py:242
Async XLA Ops:
  1.4 1.7 %copy-start = (bf16[3,640,640]{2,1,0:T(8,128)(2,1)S(1)}, bf16[3,640,640]{2,1,0:T(8,128)(2,1)}, u32[]{:S(2)}) copy-start(bf16[3,640,640]{2,1,0:T(8,128)(2,1)} %inverse_hbm.1) | copy-start | bytes 7372804
  3.1 1.5 %copy-start.1 = (bf16[3,640,512]{2,1,0:T(8,128)(2,1)S(1)}, bf16[3,640,512]{2,1,0:T(8,128)(2,1)}, u32[]{:S(2)}) copy-start(bf16[3,640,512]{2,1,0:T(8,128)(2,1)} %coupling_hbm.1) | copy-start | bytes 5898244
  4.6 0.7 copy-start.2
  5.3 0.7 copy-start.3
  6.0 0.7 copy-start.4
  6.7 0.7 copy-start.6
  15.8 53.3 %copy-start.5 = (s32[1,256]{1,0:T(1,128)S(1)}, s32[1,256]{1,0:T(1,128)}, u32[]{:S(2)}) copy-start(s32[1,256]{1,0:T(1,128)} %target_ref.1) | copy-start | bytes 3076

commit v2 on v1

v2 whole, which is shorter than its diff:
```python
import jax
import jax.numpy as jnp
from jax import lax
from jax.experimental import pallas as pl
from jax.experimental.pallas import tpu as pltpu
from jax.sharding import PartitionSpec as P

PR = 128
NPS = 4
P_OWN = 4
CAP = 3
N_Z = 16
N_Y = 4
BITS = 2
SHARE = N_Z * BITS
CHUNK = CAP * SHARE + 8
CODE_ROW = CAP
LOADS = SHARE * P_OWN
BACK = N_Y * P_OWN * BITS + 8
VMEM_LIMIT = 40 * 1024 * 1024


def iota(shape, axis):
    return lax.broadcasted_iota(jnp.int32, shape, axis)


def condense_kernel(
    ply_hbm,
    slot_hbm,
    inverse_hbm,
    coupling_hbm,
    stiffness_hbm,
    interior_hbm,
    boundary_hbm,
    out_ref,
    ply_ref,
    slot_ref,
    inverse_buf,
    coupling_buf,
    stiffness_ref,
    interior_ref,
    boundary_ref,
    rows_ref,
    extra,
    count,
    sems,
    small_sems,
):
    subs, inner_size, width = coupling_buf.shape
    plies = extra.shape[0]
    small = [
        pltpu.make_async_copy(source, target, small_sems.at[n])
        for n, (source, target) in enumerate(
            (
                (ply_hbm, ply_ref),
                (slot_hbm, slot_ref),
                (stiffness_hbm, stiffness_ref),
                (interior_hbm, interior_ref),
                (boundary_hbm, boundary_ref),
            )
        )
    ]
    for copy in small:
        copy.start()

    def sub_copies(s):
        return (
            pltpu.make_async_copy(inverse_hbm.at[s], inverse_buf.at[s], sems.at[0, s]),
            pltpu.make_async_copy(coupling_hbm.at[s], coupling_buf.at[s], sems.at[1, s]),
        )

    for s in range(subs):
        for copy in sub_copies(s):
            copy.start()
    out_ref[...] = jnp.zeros_like(out_ref)
    extra[...] = jnp.where(iota(extra.shape, 1) == CODE_ROW, -1.0, 0.0)
    for q in range(plies):
        count[q] = 0
    lane = iota((1, PR), 1)
    row_code = (lane % N_Z) * (BITS * P_OWN) + ((lane // N_Z) % BITS) * P_OWN
    row_item = lane // SHARE
    row = iota((PR, PR), 0)
    source = (row % N_Z) * (N_Y * BITS) + (row // SHARE) * BITS + (row // N_Z) % BITS
    ordered = source == iota((PR, PR), 1)
    wide_row = iota((2 * PR, 2 * PR), 0)
    wide_source = (
        (wide_row % N_Z) * (N_Y * BITS)
        + (wide_row % PR // SHARE) * BITS
        + (wide_row // N_Z) % BITS
        + wide_row // PR * PR
    )
    order = (wide_source == iota((2 * PR, 2 * PR), 1)).astype(jnp.bfloat16)
    for copy in small:
        copy.wait()
    rows_ref[0:subs, 0:width] = stiffness_ref[...].astype(jnp.float32)
    rows_ref[8 : 8 + subs, 0:inner_size] = interior_ref[...].astype(jnp.float32)
    rows_ref[16 : 16 + subs, 0:width] = boundary_ref[...].astype(jnp.float32)

    def subregion(s, carry):
        for copy in sub_copies(s):
            copy.wait()
        stiffness = rows_ref[pl.ds(s, 1), 0:width]
        interior = rows_ref[pl.ds(8 + s, 1), 0:inner_size]
        boundary = rows_ref[pl.ds(16 + s, 1), 0:width]
        load = jnp.broadcast_to(interior, (16, inner_size)).astype(jnp.bfloat16)
        solved = lax.dot_general(
            load, inverse_buf[s], (((1,), (1,)), ((), ())), preferred_element_type=jnp.float32
        ).astype(jnp.bfloat16)
        left = jnp.concatenate([inverse_buf[s], solved], axis=0)
        for pair in range(width // (2 * PR)):
            columns = coupling_buf[s, :, pair * 2 * PR : (pair + 1) * 2 * PR]
            turned = lax.dot_general(
                order, columns, (((1,), (1,)), ((), ())), preferred_element_type=jnp.float32
            ).astype(jnp.bfloat16)
            both = jnp.dot(left, columns, preferred_element_type=jnp.float32)
            inner = both[0:inner_size].astype(jnp.bfloat16)
            condensed = (
                boundary[:, pair * 2 * PR : (pair + 1) * 2 * PR]
                - both[inner_size : inner_size + 1]
            )
            condensed = condensed.astype(jnp.bfloat16).astype(jnp.float32)
            product = jnp.dot(turned, inner, preferred_element_type=jnp.float32)
            for half in range(2):
                k = pair * 2 + half
                item = s * NPS + k
                block = product[half * PR : (half + 1) * PR, half * PR : (half + 1) * PR]
                diagonal = jnp.where(ordered, stiffness[:, k * PR : (k + 1) * PR], 0.0)
                panel = (diagonal - block).astype(jnp.bfloat16)
                q = ply_ref[item]
                slot = slot_ref[item]
                rank = count[q]
                count[q] = rank + 1
                for y in range(N_Y):
                    out_ref[y * plies + q, pl.ds(pl.multiple_of(rank * SHARE, SHARE), SHARE), :] = (
                        panel[y * SHARE : (y + 1) * SHARE]
                    )
                extra[q, pl.ds(rank, 1), :] = condensed[:, half * PR : (half + 1) * PR]
                codes = extra[q, CODE_ROW : CODE_ROW + 1, :]
                codes = jnp.where(row_item == rank, (row_code + slot).astype(jnp.float32), codes)
                codes = jnp.where(
                    lane == CAP * SHARE + rank, (LOADS + slot).astype(jnp.float32), codes
                )
                extra[q, CODE_ROW : CODE_ROW + 1, :] = codes
        return carry

    lax.fori_loop(0, subs, subregion, 0)
    is_code = iota((8, PR), 0) == CODE_ROW
    for q in range(plies):
        rows = extra[q]
        for y in range(N_Y):
            turned = rows if y == 0 else pltpu.roll(rows, PR - BITS * y, 1)
            out_ref[y * plies + q, CAP * SHARE : CHUNK, :] = jnp.where(
                is_code, rows, turned
            ).astype(jnp.bfloat16)


def combine_kernel(got_ref, out_ref):
    plies = got_ref.shape[0] // N_Y
    sum_rows = iota((LOADS + 8, CHUNK), 0).astype(jnp.float32)
    sums = []
    for y in range(N_Y):
        total = jnp.zeros((LOADS + 8, PR), jnp.float32)
        for q in range(plies):
            message = got_ref[y * plies + q]
            tail = message[CAP * SHARE : CHUNK].astype(jnp.float32)
            codes = tail[CODE_ROW : CODE_ROW + 1, 0:CHUNK]
            choose = (sum_rows == codes).astype(jnp.bfloat16)
            total = total + jnp.dot(choose, message, preferred_element_type=jnp.float32)
        sums.append(total)
    loads = jnp.concatenate([t[LOADS : LOADS + P_OWN] for t in sums], axis=0)
    loads = jnp.concatenate([loads, jnp.zeros((PR - N_Y * P_OWN, PR), jnp.float32)], axis=0)
    loads = loads.T
    step = BITS * P_OWN
    for z in range(N_Z):
        rows = [t[z * step : (z + 1) * step] for t in sums] + [loads[z * step : (z + 1) * step]]
        out_ref[z] = jnp.concatenate(rows, axis=0).astype(jnp.bfloat16)


def place_kernel(target_ref, got_ref, blocks_ref, loads_ref):
    patches = target_ref.shape[1]
    target = target_ref[...]
    rows = N_Y * P_OWN * BITS
    slots = P_OWN - 1
    blocks = got_ref[:, 0:rows, :].reshape(N_Z * rows, PR)
    loads = got_ref[:, rows:BACK, :].astype(jnp.float32).reshape(N_Z * 8, PR)
    loads = loads.astype(jnp.bfloat16)
    for bit in range(BITS):
        wanted = (target - (target & slots)) * BITS + bit * P_OWN + (target & slots)
        choose = (iota((N_Z * rows, patches), 0) == wanted).astype(jnp.bfloat16)
        blocks_ref[0, bit] = lax.dot_general(
            choose, blocks, (((0,), (0,)), ((), ())), preferred_element_type=jnp.float32
        )
        wanted = (target // (N_Y * P_OWN)) * 8 + bit
        choose = (iota((N_Z * 8, patches), 0) == wanted).astype(jnp.bfloat16)
        picked = lax.dot_general(
            loads, choose, (((0,), (0,)), ((), ())), preferred_element_type=jnp.float32
        )[0 : N_Y * P_OWN]
        mine = iota(picked.shape, 0) == target % (N_Y * P_OWN)
        loads_ref[0, bit : bit + 1, :] = jnp.sum(
            jnp.where(mine, picked, 0.0), axis=0, keepdims=True
        )


def vmem():
    return pl.BlockSpec(memory_space=pltpu.VMEM)


def condense(*arguments):
    touch_slot, interior_inverse, coupling = arguments[1:4]
    subs, inner_size, width = coupling.shape
    plies = lax.axis_size("ply")
    return pl.pallas_call(
        condense_kernel,
        out_shape=jax.ShapeDtypeStruct((N_Y * plies, CHUNK, PR), jnp.bfloat16),
        in_specs=[pl.BlockSpec(memory_space=pltpu.HBM)] * len(arguments),
        out_specs=vmem(),
        scratch_shapes=[
            pltpu.SMEM(touch_slot.shape, jnp.int32),
            pltpu.SMEM(touch_slot.shape, jnp.int32),
            pltpu.VMEM(interior_inverse.shape, jnp.bfloat16),
            pltpu.VMEM(coupling.shape, jnp.bfloat16),
            pltpu.VMEM((subs, width), jnp.bfloat16),
            pltpu.VMEM((subs, inner_size), jnp.bfloat16),
            pltpu.VMEM((subs, width), jnp.bfloat16),
            pltpu.VMEM((24, inner_size), jnp.float32),
            pltpu.VMEM((plies, 8, PR), jnp.float32),
            pltpu.SMEM((plies,), jnp.int32),
            pltpu.SemaphoreType.DMA((2, subs)),
            pltpu.SemaphoreType.DMA((5,)),
        ],
        compiler_params=pltpu.CompilerParams(vmem_limit_bytes=VMEM_LIMIT),
        name="condense",
    )(*(pltpu.with_memory_space_constraint(argument, pltpu.HBM) for argument in arguments))


def combine(got):
    return pl.pallas_call(
        combine_kernel,
        out_shape=jax.ShapeDtypeStruct((N_Z, BACK, PR), jnp.bfloat16),
        in_specs=[vmem()],
        out_specs=vmem(),
        compiler_params=pltpu.CompilerParams(vmem_limit_bytes=VMEM_LIMIT),
        name="combine",
    )(got)


def place(target, got):
    patches = target.shape[1]
    return pl.pallas_call(
        place_kernel,
        out_shape=(
            jax.ShapeDtypeStruct((1, BITS, patches, PR), jnp.float32),
            jax.ShapeDtypeStruct((1, BITS, patches), jnp.float32),
        ),
        in_specs=[vmem(), vmem()],
        out_specs=(vmem(), vmem()),
        compiler_params=pltpu.CompilerParams(vmem_limit_bytes=VMEM_LIMIT),
        name="place",
    )(target, got)


def on_device(
    interior_inverse,
    coupling,
    boundary_stiffness,
    interior_load,
    boundary_load,
    touch_ply,
    touch_slot,
    source_position,
):
    send = condense(
        touch_ply.reshape(-1),
        touch_slot,
        interior_inverse,
        coupling,
        boundary_stiffness,
        interior_load,
        boundary_load,
    )
    plane = N_Y * lax.axis_size("ply")
    got = lax.all_to_all(
        send,
        ("wide", "ply"),
        split_axis=0,
        concat_axis=0,
        tiled=True,
        axis_index_groups=[[z * plane + i for i in range(plane)] for z in range(N_Z)],
    )
    got = lax.all_to_all(
        combine(got),
        "wide",
        split_axis=0,
        concat_axis=0,
        tiled=True,
        axis_index_groups=[[z * N_Y + y for z in range(N_Z)] for y in range(N_Y)],
    )
    return place(source_position, got)


def solution(mesh):
    return jax.shard_map(
        on_device,
        mesh=mesh,
        in_specs=(
            P(("wide", "ply"), None, None),
            P(("wide", "ply"), None, None),
            P(("wide", "ply"), None),
            P(("wide", "ply"), None),
            P(("wide", "ply"), None),
            P(("wide", "ply"), None),
            P(("wide", "ply")),
            P("ply", None),
        ),
        out_specs=(P("ply", "wide", None, None), P("ply", "wide", None)),
        check_vma=False,
    )
```

time: 70.5 us -> 63.4 us (0.90)
  local copies, waits for them, and re-layouts: 6.7 us -> 0.01 us
    unnamed x15 -> x2, local copies, waits for them, and re-layouts: 6.7 us -> 0.01 us
where the time goes in v2:
time: 63.4 us; the launch traced here: 63.2 us
  blocking collectives  52.4 us (83%)
  Pallas kernels  10.1 us (16%)
  between operations  0.66 us (1%)
    all_to_all x1, blocking collectives, on_device(): lax.all_to_all(combine(got), 'wide', split_axis=0, concat_axis=0, tiled=T...  30.1 us
    all_to_all x1, blocking collectives, on_device(): lax.all_to_all(send, ('wide', 'ply'), split_axis=0, concat_axis=0, tiled=...  22.3 us
    pallas_call x1, Pallas kernels, condense(): pl.pallas_call(condense_kernel, out_shape=jax.ShapeDtypeStruct((N_Y * pli...  8.22 us

profile of v2, /device:TPU:32, one launch (start us, length us, event | category | flops | bytes accessed | tf_op | source)
XLA Modules:
  0.0 63.2 jit_solution(13484707432086148475)
XLA Ops:
  0.6 8.2 %condense.1 = bf16[32,104,128]{2,1,0:T(8,128)(2,1)S(1)} custom-call(s32[12]{0:T(128)} %bitcast.1, s32[12]{0:T(128)} %slot_hbm.1, bf16[3,640,640]{2,1,0:T(8,128)(2,1)} %inverse_hbm.1, bf16[3,640,512]{2,1,0:T(8,128)(2,1)} %coupling_hbm.1, bf16[3,512]{1,0:T(4,128)(2,1)} %stiffness_hbm.1, bf16[3,640]{1,0:T(4,128)(2,1)} %interior_hbm.1, bf16[3,512]{1,0:T(4,128)(2,1)} %boundary_hbm.1), custom_call_target="tpu_custom_call" | custom-call | tf_op jit(solution)/shard_map/condense/pallas_call | solution.py:212
  8.9 0.0 copy-start
  8.9 22.3 %all_to_all.10.got_ref = bf16[32,104,128]{2,1,0:T(8,128)(2,1)S(1)} all-to-all(bf16[32,104,128]{2,1,0:T(8,128)(2,1)S(1)} %condense.1), channel_id=1, replica_groups={{0,1,2,3,4,5,6,7,8,9,10,11,12,13,14,15,16,17,18,19,20,21,22,23,24,25,26..., dimensions={0} | all-to-all | bytes 1703936 | tf_op jit(solution)/shard_map/all_to_all | solution.py:282
  31.2 0.8 %combine.1 = bf16[16,40,128]{2,1,0:T(8,128)(2,1)S(1)} custom-call(bf16[32,104,128]{2,1,0:T(8,128)(2,1)S(1)} %all_to_all.10.got_ref), custom_call_target="tpu_custom_call" | custom-call | tf_op jit(solution)/shard_map/combine/pallas_call | solution.py:237
  32.1 30.1 %all_to_all.11.got_ref = bf16[16,40,128]{2,1,0:T(8,128)(2,1)S(1)} all-to-all(bf16[16,40,128]{2,1,0:T(8,128)(2,1)S(1)} %combine.1), channel_id=1, replica_groups={{0,32,64,96,128,160,192,224,256,288,320,352,384,416,448,480},{8,40,72,1..., dimensions={0} | all-to-all | bytes 327680 | tf_op jit(solution)/shard_map/all_to_all | solution.py:290
  62.1 0.0 copy-done
  62.1 1.1 %place.1 = (f32[1,2,256,128]{3,2,1,0:T(8,128)}, f32[1,2,256]{2,1,0:T(2,128)}) custom-call(s32[1,256]{1,0:T(1,128)S(1)} %copy-done, bf16[16,40,128]{2,1,0:T(8,128)(2,1)S(1)} %all_to_all.11.got_ref), custom_call_target="tpu_custom_call" | custom-call | tf_op jit(solution)/shard_map/place/pallas_call | solution.py:249
Async XLA Ops:
  8.9 53.3 %copy-start = (s32[1,256]{1,0:T(1,128)S(1)}, s32[1,256]{1,0:T(1,128)}, u32[]{:S(2)}) copy-start(s32[1,256]{1,0:T(1,128)} %target_ref.1) | copy-start | bytes 3076

commit v3 on v2

--- a/solution.py
+++ b/solution.py
@@ -41,6 +41,7 @@
     interior_ref,
     boundary_ref,
     rows_ref,
+    panels,
     extra,
     count,
     sems,
@@ -60,18 +61,14 @@
             )
         )
     ]
-    for copy in small:
-        copy.start()
-
     def sub_copies(s):
         return (
             pltpu.make_async_copy(inverse_hbm.at[s], inverse_buf.at[s], sems.at[0, s]),
             pltpu.make_async_copy(coupling_hbm.at[s], coupling_buf.at[s], sems.at[1, s]),
         )
 
-    for s in range(subs):
-        for copy in sub_copies(s):
-            copy.start()
+    for copy in (*sub_copies(0), *small, *sub_copies(1)):
+        copy.start()
     out_ref[...] = jnp.zeros_like(out_ref)
     extra[...] = jnp.where(iota(extra.shape, 1) == CODE_ROW, -1.0, 0.0)
     for q in range(plies):
@@ -79,17 +76,7 @@
     lane = iota((1, PR), 1)
     row_code = (lane % N_Z) * (BITS * P_OWN) + ((lane // N_Z) % BITS) * P_OWN
     row_item = lane // SHARE
-    row = iota((PR, PR), 0)
-    source = (row % N_Z) * (N_Y * BITS) + (row // SHARE) * BITS + (row // N_Z) % BITS
-    ordered = source == iota((PR, PR), 1)
-    wide_row = iota((2 * PR, 2 * PR), 0)
-    wide_source = (
-        (wide_row % N_Z) * (N_Y * BITS)
-        + (wide_row % PR // SHARE) * BITS
-        + (wide_row // N_Z) % BITS
-        + wide_row // PR * PR
-    )
-    order = (wide_source == iota((2 * PR, 2 * PR), 1)).astype(jnp.bfloat16)
+    same = iota((PR, PR), 0) == iota((PR, PR), 1)
     for copy in small:
         copy.wait()
     rows_ref[0:subs, 0:width] = stiffness_ref[...].astype(jnp.float32)
@@ -99,48 +86,51 @@
     def subregion(s, carry):
         for copy in sub_copies(s):
             copy.wait()
+
+        @pl.when(s + 2 < subs)
+        def _():
+            for copy in sub_copies(s + 2):
+                copy.start()
+
         stiffness = rows_ref[pl.ds(s, 1), 0:width]
         interior = rows_ref[pl.ds(8 + s, 1), 0:inner_size]
         boundary = rows_ref[pl.ds(16 + s, 1), 0:width]
-        load = jnp.broadcast_to(interior, (16, inner_size)).astype(jnp.bfloat16)
-        solved = lax.dot_general(
-            load, inverse_buf[s], (((1,), (1,)), ((), ())), preferred_element_type=jnp.float32
-        ).astype(jnp.bfloat16)
-        left = jnp.concatenate([inverse_buf[s], solved], axis=0)
-        for pair in range(width // (2 * PR)):
-            columns = coupling_buf[s, :, pair * 2 * PR : (pair + 1) * 2 * PR]
-            turned = lax.dot_general(
-                order, columns, (((1,), (1,)), ((), ())), preferred_element_type=jnp.float32
-            ).astype(jnp.bfloat16)
-            both = jnp.dot(left, columns, preferred_element_type=jnp.float32)
-            inner = both[0:inner_size].astype(jnp.bfloat16)
-            condensed = (
-                boundary[:, pair * 2 * PR : (pair + 1) * 2 * PR]
-                - both[inner_size : inner_size + 1]
+        inverse = inverse_buf[s]
+        coupling = coupling_buf[s]
+        turned = coupling.T
+        solved = jnp.sum(inverse.astype(jnp.float32) * interior, axis=1, keepdims=True)
+        solved = solved.astype(jnp.bfloat16).astype(jnp.float32)
+        inner = jnp.dot(inverse, coupling, preferred_element_type=jnp.float32)
+        inner = inner.astype(jnp.bfloat16)
+        carried = jnp.sum(coupling.astype(jnp.float32) * solved, axis=0, keepdims=True)
+        condensed = (boundary - carried).astype(jnp.bfloat16).astype(jnp.float32)
+        for k in range(NPS):
+            columns = slice(k * PR, (k + 1) * PR)
+            product = jnp.dot(
+                turned[columns], inner[:, columns], preferred_element_type=jnp.float32
             )
-            condensed = condensed.astype(jnp.bfloat16).astype(jnp.float32)
-            product = jnp.dot(turned, inner, preferred_element_type=jnp.float32)
-            for half in range(2):
-                k = pair * 2 + half
-                item = s * NPS + k
-                block = product[half * PR : (half + 1) * PR, half * PR : (half + 1) * PR]
-                diagonal = jnp.where(ordered, stiffness[:, k * PR : (k + 1) * PR], 0.0)
-                panel = (diagonal - block).astype(jnp.bfloat16)
-                q = ply_ref[item]
-                slot = slot_ref[item]
-                rank = count[q]
-                count[q] = rank + 1
-                for y in range(N_Y):
-                    out_ref[y * plies + q, pl.ds(pl.multiple_of(rank * SHARE, SHARE), SHARE), :] = (
-                        panel[y * SHARE : (y + 1) * SHARE]
-                    )
-                extra[q, pl.ds(rank, 1), :] = condensed[:, half * PR : (half + 1) * PR]
-                codes = extra[q, CODE_ROW : CODE_ROW + 1, :]
-                codes = jnp.where(row_item == rank, (row_code + slot).astype(jnp.float32), codes)
-                codes = jnp.where(
-                    lane == CAP * SHARE + rank, (LOADS + slot).astype(jnp.float32), codes
+            panels[columns, :] = jnp.where(same, stiffness[:, columns], 0.0) - product
+        for k in range(NPS):
+            item = s * NPS + k
+            q = ply_ref[item]
+            slot = slot_ref[item]
+            rank = count[q]
+            count[q] = rank + 1
+            for y in range(N_Y):
+                part = [
+                    panels[pl.ds(k * PR + y * BITS + bit, N_Z, stride=N_Y * BITS), :]
+                    for bit in range(BITS)
+                ]
+                out_ref[y * plies + q, pl.ds(pl.multiple_of(rank * SHARE, SHARE), SHARE), :] = (
+                    jnp.concatenate(part, axis=0).astype(jnp.bfloat16)
                 )
-                extra[q, CODE_ROW : CODE_ROW + 1, :] = codes
+            extra[q, pl.ds(rank, 1), :] = condensed[:, k * PR : (k + 1) * PR]
+            codes = extra[q, CODE_ROW : CODE_ROW + 1, :]
+            codes = jnp.where(row_item == rank, (row_code + slot).astype(jnp.float32), codes)
+            codes = jnp.where(
+                lane == CAP * SHARE + rank, (LOADS + slot).astype(jnp.float32), codes
+            )
+            extra[q, CODE_ROW : CODE_ROW + 1, :] = codes
         return carry
 
     lax.fori_loop(0, subs, subregion, 0)
@@ -223,6 +213,7 @@
             pltpu.VMEM((subs, inner_size), jnp.bfloat16),
             pltpu.VMEM((subs, width), jnp.bfloat16),
             pltpu.VMEM((24, inner_size), jnp.float32),
+            pltpu.VMEM((width, PR), jnp.float32),
             pltpu.VMEM((plies, 8, PR), jnp.float32),
             pltpu.SMEM((plies,), jnp.int32),
             pltpu.SemaphoreType.DMA((2, subs)),

time: 63.4 us -> 60 us (0.946)
  Pallas kernels: 10.1 us -> 6.7 us
    pallas_call x1, Pallas kernels: 8.22 us -> 4.78 us  [condense(): pl.pallas_call(condense_kernel, out_shape=jax.ShapeDtypeStruct((N_Y * pli...]
where the time goes in v3:
time: 60 us; the launch traced here: 59.8 us
  blocking collectives  52.4 us (87%)
  Pallas kernels  6.7 us (11%)
  between operations  0.66 us (1%)
    all_to_all x1, blocking collectives, on_device(): lax.all_to_all(combine(got), 'wide', split_axis=0, concat_axis=0, tiled=T...  30.1 us
    all_to_all x1, blocking collectives, on_device(): lax.all_to_all(send, ('wide', 'ply'), split_axis=0, concat_axis=0, tiled=...  22.3 us
    pallas_call x1, Pallas kernels, condense(): pl.pallas_call(condense_kernel, out_shape=jax.ShapeDtypeStruct((N_Y * pli...  4.78 us

profile of v3, /device:TPU:32, one launch (start us, length us, event | category | flops | bytes accessed | tf_op | source)
XLA Modules:
  0.0 59.8 jit_solution(4438437464867277306)
XLA Ops:
  0.6 4.8 %condense.1 = bf16[32,104,128]{2,1,0:T(8,128)(2,1)S(1)} custom-call(s32[12]{0:T(128)} %bitcast.1, s32[12]{0:T(128)} %slot_hbm.1, bf16[3,640,640]{2,1,0:T(8,128)(2,1)} %inverse_hbm.1, bf16[3,640,512]{2,1,0:T(8,128)(2,1)} %coupling_hbm.1, bf16[3,512]{1,0:T(4,128)(2,1)} %stiffness_hbm.1, bf16[3,640]{1,0:T(4,128)(2,1)} %interior_hbm.1, bf16[3,512]{1,0:T(4,128)(2,1)} %boundary_hbm.1), custom_call_target="tpu_custom_call" | custom-call | tf_op jit(solution)/shard_map/condense/pallas_call | solution.py:202
  5.4 0.0 copy-start
  5.4 22.3 %all_to_all.10.got_ref = bf16[32,104,128]{2,1,0:T(8,128)(2,1)S(1)} all-to-all(bf16[32,104,128]{2,1,0:T(8,128)(2,1)S(1)} %condense.1), channel_id=1, replica_groups={{0,1,2,3,4,5,6,7,8,9,10,11,12,13,14,15,16,17,18,19,20,21,22,23,24,25,26..., dimensions={0} | all-to-all | bytes 1703936 | tf_op jit(solution)/shard_map/all_to_all | solution.py:273
  27.8 0.8 %combine.1 = bf16[16,40,128]{2,1,0:T(8,128)(2,1)S(1)} custom-call(bf16[32,104,128]{2,1,0:T(8,128)(2,1)S(1)} %all_to_all.10.got_ref), custom_call_target="tpu_custom_call" | custom-call | tf_op jit(solution)/shard_map/combine/pallas_call | solution.py:228
  28.6 30.1 %all_to_all.11.got_ref = bf16[16,40,128]{2,1,0:T(8,128)(2,1)S(1)} all-to-all(bf16[16,40,128]{2,1,0:T(8,128)(2,1)S(1)} %combine.1), channel_id=1, replica_groups={{0,32,64,96,128,160,192,224,256,288,320,352,384,416,448,480},{8,40,72,1..., dimensions={0} | all-to-all | bytes 327680 | tf_op jit(solution)/shard_map/all_to_all | solution.py:281
  58.7 0.0 copy-done
  58.7 1.1 %place.1 = (f32[1,2,256,128]{3,2,1,0:T(8,128)}, f32[1,2,256]{2,1,0:T(2,128)}) custom-call(s32[1,256]{1,0:T(1,128)S(1)} %copy-done, bf16[16,40,128]{2,1,0:T(8,128)(2,1)S(1)} %all_to_all.11.got_ref), custom_call_target="tpu_custom_call" | custom-call | tf_op jit(solution)/shard_map/place/pallas_call | solution.py:240
Async XLA Ops:
  5.4 53.3 %copy-start = (s32[1,256]{1,0:T(1,128)S(1)}, s32[1,256]{1,0:T(1,128)}, u32[]{:S(2)}) copy-start(s32[1,256]{1,0:T(1,128)} %target_ref.1) | copy-start | bytes 3076

commit v4 on v3

--- a/solution.py
+++ b/solution.py
@@ -17,6 +17,8 @@
 CODE_ROW = CAP
 LOADS = SHARE * P_OWN
 BACK = N_Y * P_OWN * BITS + 8
+FIRST_Z = 10
+LAST = 11
 VMEM_LIMIT = 40 * 1024 * 1024
 
 
@@ -121,7 +123,8 @@
                     panels[pl.ds(k * PR + y * BITS + bit, N_Z, stride=N_Y * BITS), :]
                     for bit in range(BITS)
                 ]
-                out_ref[y * plies + q, pl.ds(pl.multiple_of(rank * SHARE, SHARE), SHARE), :] = (
+                place = lax.rem(y * plies + q + LAST, N_Y * plies)
+                out_ref[place, pl.ds(pl.multiple_of(rank * SHARE, SHARE), SHARE), :] = (
                     jnp.concatenate(part, axis=0).astype(jnp.bfloat16)
                 )
             extra[q, pl.ds(rank, 1), :] = condensed[:, k * PR : (k + 1) * PR]
@@ -139,7 +142,8 @@
         rows = extra[q]
         for y in range(N_Y):
             turned = rows if y == 0 else pltpu.roll(rows, PR - BITS * y, 1)
-            out_ref[y * plies + q, CAP * SHARE : CHUNK, :] = jnp.where(
+            place = (y * plies + q + LAST) % (N_Y * plies)
+            out_ref[place, CAP * SHARE : CHUNK, :] = jnp.where(
                 is_code, rows, turned
             ).astype(jnp.bfloat16)
 
@@ -151,7 +155,7 @@
     for y in range(N_Y):
         total = jnp.zeros((LOADS + 8, PR), jnp.float32)
         for q in range(plies):
-            message = got_ref[y * plies + q]
+            message = got_ref[(y * plies + q + LAST) % (N_Y * plies)]
             tail = message[CAP * SHARE : CHUNK].astype(jnp.float32)
             codes = tail[CODE_ROW : CODE_ROW + 1, 0:CHUNK]
             choose = (sum_rows == codes).astype(jnp.bfloat16)
@@ -163,12 +167,13 @@
     step = BITS * P_OWN
     for z in range(N_Z):
         rows = [t[z * step : (z + 1) * step] for t in sums] + [loads[z * step : (z + 1) * step]]
-        out_ref[z] = jnp.concatenate(rows, axis=0).astype(jnp.bfloat16)
+        out_ref[(z - FIRST_Z) % N_Z] = jnp.concatenate(rows, axis=0).astype(jnp.bfloat16)
 
 
 def place_kernel(target_ref, got_ref, blocks_ref, loads_ref):
     patches = target_ref.shape[1]
-    target = target_ref[...]
+    z_owners = N_Y * P_OWN
+    target = lax.rem(target_ref[...] + (N_Z - FIRST_Z) * z_owners, N_Z * z_owners)
     rows = N_Y * P_OWN * BITS
     slots = P_OWN - 1
     blocks = got_ref[:, 0:rows, :].reshape(N_Z * rows, PR)
@@ -180,12 +185,12 @@
         blocks_ref[0, bit] = lax.dot_general(
             choose, blocks, (((0,), (0,)), ((), ())), preferred_element_type=jnp.float32
         )
-        wanted = (target // (N_Y * P_OWN)) * 8 + bit
+        wanted = (target // z_owners) * 8 + bit
         choose = (iota((N_Z * 8, patches), 0) == wanted).astype(jnp.bfloat16)
         picked = lax.dot_general(
             loads, choose, (((0,), (0,)), ((), ())), preferred_element_type=jnp.float32
-        )[0 : N_Y * P_OWN]
-        mine = iota(picked.shape, 0) == target % (N_Y * P_OWN)
+        )[0:z_owners]
+        mine = iota(picked.shape, 0) == target % z_owners
         loads_ref[0, bit : bit + 1, :] = jnp.sum(
             jnp.where(mine, picked, 0.0), axis=0, keepdims=True
         )
@@ -276,7 +281,9 @@
         split_axis=0,
         concat_axis=0,
         tiled=True,
-        axis_index_groups=[[z * plane + i for i in range(plane)] for z in range(N_Z)],
+        axis_index_groups=[
+            [z * plane + (i - LAST) % plane for i in range(plane)] for z in range(N_Z)
+        ],
     )
     got = lax.all_to_all(
         combine(got),
@@ -284,7 +291,9 @@
         split_axis=0,
         concat_axis=0,
         tiled=True,
-        axis_index_groups=[[z * N_Y + y for z in range(N_Z)] for y in range(N_Y)],
+        axis_index_groups=[
+            [(i + FIRST_Z) % N_Z * N_Y + y for i in range(N_Z)] for y in range(N_Y)
+        ],
     )
     return place(source_position, got)
 

time: 60 us -> 53.3 us (0.89)
  the two profiles are of different devices: /device:TPU:32 before, /device:TPU:1 now
where the time goes in v4:
time: 53.3 us; the launch traced here: 52.6 us
  blocking collectives  45.2 us (85%)
  Pallas kernels  6.77 us (13%)
  between operations  0.66 us (1%)
    all_to_all x1, blocking collectives, on_device(): lax.all_to_all(send, ('wide', 'ply'), split_axis=0, concat_axis=0, tiled=...  23.9 us
    all_to_all x1, blocking collectives, on_device(): lax.all_to_all(combine(got), 'wide', split_axis=0, concat_axis=0, tiled=T...  21.3 us
    pallas_call x1, Pallas kernels, condense(): pl.pallas_call(condense_kernel, out_shape=jax.ShapeDtypeStruct((N_Y * pli...  4.85 us
    pallas_call x1, Pallas kernels, place(): pl.pallas_call(place_kernel, out_shape=(jax.ShapeDtypeStruct((1, BITS, pa...  1.08 us

profile of v4, /device:TPU:1, one launch (start us, length us, event | category | flops | bytes accessed | tf_op | source)
XLA Modules:
  0.0 52.6 jit_solution(4433424266310687272)
XLA Ops:
  0.6 4.8 %condense.1 = bf16[32,104,128]{2,1,0:T(8,128)(2,1)S(1)} custom-call(s32[12]{0:T(128)} %bitcast.1, s32[12]{0:T(128)} %slot_hbm.1, bf16[3,640,640]{2,1,0:T(8,128)(2,1)} %inverse_hbm.1, bf16[3,640,512]{2,1,0:T(8,128)(2,1)} %coupling_hbm.1, bf16[3,512]{1,0:T(4,128)(2,1)} %stiffness_hbm.1, bf16[3,640]{1,0:T(4,128)(2,1)} %interior_hbm.1, bf16[3,512]{1,0:T(4,128)(2,1)} %boundary_hbm.1), custom_call_target="tpu_custom_call" | custom-call | tf_op jit(solution)/shard_map/condense/pallas_call | solution.py:207
  5.5 0.0 copy-start
  5.5 23.9 %all_to_all.10.got_ref = bf16[32,104,128]{2,1,0:T(8,128)(2,1)S(1)} all-to-all(bf16[32,104,128]{2,1,0:T(8,128)(2,1)S(1)} %condense.1), channel_id=1, replica_groups={{21,22,23,24,25,26,27,28,29,30,31,0,1,2,3,4,5,6,7,8,9,10,11,12,13,14,15..., dimensions={0} | all-to-all | bytes 1703936 | tf_op jit(solution)/shard_map/all_to_all | solution.py:278
  29.4 0.8 %combine.1 = bf16[16,40,128]{2,1,0:T(8,128)(2,1)S(1)} custom-call(bf16[32,104,128]{2,1,0:T(8,128)(2,1)S(1)} %all_to_all.10.got_ref), custom_call_target="tpu_custom_call" | custom-call | tf_op jit(solution)/shard_map/combine/pallas_call | solution.py:233
  30.2 21.3 %all_to_all.11.got_ref = bf16[16,40,128]{2,1,0:T(8,128)(2,1)S(1)} all-to-all(bf16[16,40,128]{2,1,0:T(8,128)(2,1)S(1)} %combine.1), channel_id=1, replica_groups={{320,352,384,416,448,480,0,32,64,96,128,160,192,224,256,288},{328,360,3..., dimensions={0} | all-to-all | bytes 327680 | tf_op jit(solution)/shard_map/all_to_all | solution.py:288
  51.6 0.0 copy-done
  51.6 1.1 %place.1 = (f32[1,2,256,128]{3,2,1,0:T(8,128)}, f32[1,2,256]{2,1,0:T(2,128)}) custom-call(s32[1,256]{1,0:T(1,128)S(1)} %copy-done, bf16[16,40,128]{2,1,0:T(8,128)(2,1)S(1)} %all_to_all.11.got_ref), custom_call_target="tpu_custom_call" | custom-call | tf_op jit(solution)/shard_map/place/pallas_call | solution.py:245
Async XLA Ops:
  5.5 46.1 %copy-start = (s32[1,256]{1,0:T(1,128)S(1)}, s32[1,256]{1,0:T(1,128)}, u32[]{:S(2)}) copy-start(s32[1,256]{1,0:T(1,128)} %target_ref.1) | copy-start | bytes 3076

commit v5 on v4

--- a/solution.py
+++ b/solution.py
@@ -16,7 +16,8 @@
 CHUNK = CAP * SHARE + 8
 CODE_ROW = CAP
 LOADS = SHARE * P_OWN
-BACK = N_Y * P_OWN * BITS + 8
+QUAD = 4
+BACK = N_Y * P_OWN * BITS + QUAD
 FIRST_Z = 10
 LAST = 11
 VMEM_LIMIT = 40 * 1024 * 1024
@@ -150,43 +151,57 @@
 
 def combine_kernel(got_ref, out_ref):
     plies = got_ref.shape[0] // N_Y
-    sum_rows = iota((LOADS + 8, CHUNK), 0).astype(jnp.float32)
+    sum_rows = iota((LOADS + 8, plies * PR), 0).astype(jnp.float32)
     sums = []
     for y in range(N_Y):
-        total = jnp.zeros((LOADS + 8, PR), jnp.float32)
-        for q in range(plies):
-            message = got_ref[(y * plies + q + LAST) % (N_Y * plies)]
-            tail = message[CAP * SHARE : CHUNK].astype(jnp.float32)
-            codes = tail[CODE_ROW : CODE_ROW + 1, 0:CHUNK]
-            choose = (sum_rows == codes).astype(jnp.bfloat16)
-            total = total + jnp.dot(choose, message, preferred_element_type=jnp.float32)
-        sums.append(total)
+        messages = [got_ref[(y * plies + q + LAST) % (N_Y * plies)] for q in range(plies)]
+        codes = jnp.concatenate(
+            [
+                m[CAP * SHARE : CHUNK].astype(jnp.float32)[CODE_ROW : CODE_ROW + 1]
+                for m in messages
+            ],
+            axis=1,
+        )
+        choose = (sum_rows == codes).astype(jnp.bfloat16)
+        pad = jnp.zeros((PR - CHUNK, PR), jnp.bfloat16)
+        rows = jnp.concatenate([v for m in messages for v in (m, pad)], axis=0)
+        sums.append(jnp.dot(choose, rows, preferred_element_type=jnp.float32))
     loads = jnp.concatenate([t[LOADS : LOADS + P_OWN] for t in sums], axis=0)
     loads = jnp.concatenate([loads, jnp.zeros((PR - N_Y * P_OWN, PR), jnp.float32)], axis=0)
     loads = loads.T
     step = BITS * P_OWN
     for z in range(N_Z):
-        rows = [t[z * step : (z + 1) * step] for t in sums] + [loads[z * step : (z + 1) * step]]
-        out_ref[(z - FIRST_Z) % N_Z] = jnp.concatenate(rows, axis=0).astype(jnp.bfloat16)
-
-
-def place_kernel(target_ref, got_ref, blocks_ref, loads_ref):
+        place = (z - FIRST_Z) % N_Z
+        rows = [t[z * step : (z + 1) * step] for t in sums] + [loads[z * step : z * step + QUAD]]
+        for n, row in enumerate(rows):
+            for half in range(row.shape[0] // QUAD):
+                out_ref[place, n * (step // QUAD) + half] = row[
+                    half * QUAD : (half + 1) * QUAD
+                ].astype(jnp.bfloat16)
+
+
+def place_kernel(target_ref, got_ref, blocks_ref, loads_ref, got_blocks, got_loads):
     patches = target_ref.shape[1]
     z_owners = N_Y * P_OWN
     target = lax.rem(target_ref[...] + (N_Z - FIRST_Z) * z_owners, N_Z * z_owners)
     rows = N_Y * P_OWN * BITS
-    slots = P_OWN - 1
-    blocks = got_ref[:, 0:rows, :].reshape(N_Z * rows, PR)
-    loads = got_ref[:, rows:BACK, :].astype(jnp.float32).reshape(N_Z * 8, PR)
-    loads = loads.astype(jnp.bfloat16)
+    got_loads[...] = jnp.zeros_like(got_loads)
+    for z in range(N_Z):
+        for n in range(rows // QUAD):
+            owner = z * z_owners + n // BITS * QUAD
+            got_blocks[n % BITS, owner : owner + QUAD, :] = got_ref[z, n].astype(jnp.float32)
+        got_loads[z * 8 : z * 8 + QUAD, :] = got_ref[z, rows // QUAD].astype(jnp.float32)
+    loads = got_loads[...].astype(jnp.bfloat16)
+    choose_owner = jnp.where(iota((patches, patches), 0) == target, 1.0, 0.0).astype(jnp.bfloat16)
     for bit in range(BITS):
-        wanted = (target - (target & slots)) * BITS + bit * P_OWN + (target & slots)
-        choose = (iota((N_Z * rows, patches), 0) == wanted).astype(jnp.bfloat16)
         blocks_ref[0, bit] = lax.dot_general(
-            choose, blocks, (((0,), (0,)), ((), ())), preferred_element_type=jnp.float32
+            choose_owner,
+            got_blocks[bit].astype(jnp.bfloat16),
+            (((0,), (0,)), ((), ())),
+            preferred_element_type=jnp.float32,
         )
         wanted = (target // z_owners) * 8 + bit
-        choose = (iota((N_Z * 8, patches), 0) == wanted).astype(jnp.bfloat16)
+        choose = jnp.where(iota((N_Z * 8, patches), 0) == wanted, 1.0, 0.0).astype(jnp.bfloat16)
         picked = lax.dot_general(
             loads, choose, (((0,), (0,)), ((), ())), preferred_element_type=jnp.float32
         )[0:z_owners]
@@ -232,7 +247,7 @@
 def combine(got):
     return pl.pallas_call(
         combine_kernel,
-        out_shape=jax.ShapeDtypeStruct((N_Z, BACK, PR), jnp.bfloat16),
+        out_shape=jax.ShapeDtypeStruct((N_Z, BACK // QUAD, QUAD, PR), jnp.bfloat16),
         in_specs=[vmem()],
         out_specs=vmem(),
         compiler_params=pltpu.CompilerParams(vmem_limit_bytes=VMEM_LIMIT),
@@ -250,6 +265,10 @@
         ),
         in_specs=[vmem(), vmem()],
         out_specs=(vmem(), vmem()),
+        scratch_shapes=[
+            pltpu.VMEM((BITS, patches, PR), jnp.float32),
+            pltpu.VMEM((N_Z * 8, PR), jnp.float32),
+        ],
         compiler_params=pltpu.CompilerParams(vmem_limit_bytes=VMEM_LIMIT),
         name="place",
     )(target, got)

time: 53.3 us -> 52.3 us (0.981)
  no operation moved by 1% of the time
where the time goes in v5:
time: 52.3 us; the launch traced here: 51.8 us
  blocking collectives  44.7 us (85%)
  Pallas kernels  6.43 us (12%)
  between operations  0.65 us (1%)
    all_to_all x1, blocking collectives, on_device(): lax.all_to_all(send, ('wide', 'ply'), split_axis=0, concat_axis=0, tiled=...  23.9 us
    all_to_all x1, blocking collectives, on_device(): lax.all_to_all(combine(got), 'wide', split_axis=0, concat_axis=0, tiled=T...  20.8 us
    pallas_call x1, Pallas kernels, condense(): pl.pallas_call(condense_kernel, out_shape=jax.ShapeDtypeStruct((N_Y * pli...  4.85 us

profile of v5, /device:TPU:1, one launch (start us, length us, event | category | flops | bytes accessed | tf_op | source)
XLA Modules:
  0.0 51.8 jit_solution(16323008045980752659)
XLA Ops:
  0.6 4.8 %condense.1 = bf16[32,104,128]{2,1,0:T(8,128)(2,1)S(1)} custom-call(s32[12]{0:T(128)} %bitcast.1, s32[12]{0:T(128)} %slot_hbm.1, bf16[3,640,640]{2,1,0:T(8,128)(2,1)} %inverse_hbm.1, bf16[3,640,512]{2,1,0:T(8,128)(2,1)} %coupling_hbm.1, bf16[3,512]{1,0:T(4,128)(2,1)} %stiffness_hbm.1, bf16[3,640]{1,0:T(4,128)(2,1)} %interior_hbm.1, bf16[3,512]{1,0:T(4,128)(2,1)} %boundary_hbm.1), custom_call_target="tpu_custom_call" | custom-call | tf_op jit(solution)/shard_map/condense/pallas_call | solution.py:222
  5.5 0.0 copy-start
  5.5 23.9 %all_to_all.10.got_ref = bf16[32,104,128]{2,1,0:T(8,128)(2,1)S(1)} all-to-all(bf16[32,104,128]{2,1,0:T(8,128)(2,1)S(1)} %condense.1), channel_id=1, replica_groups={{21,22,23,24,25,26,27,28,29,30,31,0,1,2,3,4,5,6,7,8,9,10,11,12,13,14,15..., dimensions={0} | all-to-all | bytes 1703936 | tf_op jit(solution)/shard_map/all_to_all | solution.py:297
  29.4 0.6 %combine.1 = bf16[16,9,4,128]{3,2,1,0:T(4,128)(2,1)S(1)} custom-call(bf16[32,104,128]{2,1,0:T(8,128)(2,1)S(1)} %all_to_all.10.got_ref), custom_call_target="tpu_custom_call" | custom-call | tf_op jit(solution)/shard_map/combine/pallas_call | solution.py:248
  29.9 20.8 %all_to_all.11.got_ref = bf16[16,9,4,128]{3,2,1,0:T(4,128)(2,1)S(1)} all-to-all(bf16[16,9,4,128]{3,2,1,0:T(4,128)(2,1)S(1)} %combine.1), channel_id=1, replica_groups={{320,352,384,416,448,480,0,32,64,96,128,160,192,224,256,288},{328,360,3..., dimensions={0} | all-to-all | bytes 294912 | tf_op jit(solution)/shard_map/all_to_all | solution.py:307
  50.7 0.0 copy-done
  50.7 1.0 %place.1 = (f32[1,2,256,128]{3,2,1,0:T(8,128)}, f32[1,2,256]{2,1,0:T(2,128)}) custom-call(s32[1,256]{1,0:T(1,128)S(1)} %copy-done, bf16[16,9,4,128]{3,2,1,0:T(4,128)(2,1)S(1)} %all_to_all.11.got_ref), custom_call_target="tpu_custom_call" | custom-call | tf_op jit(solution)/shard_map/place/pallas_call | solution.py:260
Async XLA Ops:
  5.5 45.3 %copy-start = (s32[1,256]{1,0:T(1,128)S(1)}, s32[1,256]{1,0:T(1,128)}, u32[]{:S(2)}) copy-start(s32[1,256]{1,0:T(1,128)} %target_ref.1) | copy-start | bytes 3076

commit v6 on v5

--- a/solution.py
+++ b/solution.py
@@ -8,18 +8,17 @@
 PR = 128
 NPS = 4
 P_OWN = 4
-CAP = 3
 N_Z = 16
 N_Y = 4
+CORES = 2
 BITS = 2
 SHARE = N_Z * BITS
-CHUNK = CAP * SHARE + 8
-CODE_ROW = CAP
-LOADS = SHARE * P_OWN
+LOADS = P_OWN * SHARE
+CHUNK = LOADS + 8
 QUAD = 4
 BACK = N_Y * P_OWN * BITS + QUAD
 FIRST_Z = 10
-LAST = 11
+FIRST_CHIP = 10
 VMEM_LIMIT = 40 * 1024 * 1024
 
 
@@ -35,7 +34,9 @@
     stiffness_hbm,
     interior_hbm,
     boundary_hbm,
-    out_ref,
+    sums,
+    own_loads,
+    twin_ref,
     ply_ref,
     slot_ref,
     inverse_buf,
@@ -46,12 +47,13 @@
     rows_ref,
     panels,
     extra,
-    count,
     sems,
     small_sems,
 ):
     subs, inner_size, width = coupling_buf.shape
     plies = extra.shape[0]
+    chips = twin_ref.shape[0]
+    core = lax.rem(lax.axis_index("ply"), CORES)
     small = [
         pltpu.make_async_copy(source, target, small_sems.at[n])
         for n, (source, target) in enumerate(
@@ -72,13 +74,8 @@
 
     for copy in (*sub_copies(0), *small, *sub_copies(1)):
         copy.start()
-    out_ref[...] = jnp.zeros_like(out_ref)
-    extra[...] = jnp.where(iota(extra.shape, 1) == CODE_ROW, -1.0, 0.0)
-    for q in range(plies):
-        count[q] = 0
-    lane = iota((1, PR), 1)
-    row_code = (lane % N_Z) * (BITS * P_OWN) + ((lane // N_Z) % BITS) * P_OWN
-    row_item = lane // SHARE
+    sums[...] = jnp.zeros_like(sums)
+    extra[...] = jnp.zeros_like(extra)
     same = iota((PR, PR), 0) == iota((PR, PR), 1)
     for copy in small:
         copy.wait()
@@ -117,67 +114,79 @@
             item = s * NPS + k
             q = ply_ref[item]
             slot = slot_ref[item]
-            rank = count[q]
-            count[q] = rank + 1
-            for y in range(N_Y):
-                part = [
-                    panels[pl.ds(k * PR + y * BITS + bit, N_Z, stride=N_Y * BITS), :]
-                    for bit in range(BITS)
-                ]
-                place = lax.rem(y * plies + q + LAST, N_Y * plies)
-                out_ref[place, pl.ds(pl.multiple_of(rank * SHARE, SHARE), SHARE), :] = (
-                    jnp.concatenate(part, axis=0).astype(jnp.bfloat16)
+            mine = lax.rem(q, CORES) == core
+
+            rows = pl.ds(pl.multiple_of(slot * SHARE, SHARE), SHARE)
+            places = [
+                lax.rem(y * (chips // N_Y) + q // CORES + chips - FIRST_CHIP, chips)
+                for y in range(N_Y)
+            ]
+            parts = [
+                jnp.concatenate(
+                    [
+                        panels[pl.ds(k * PR + y * BITS + bit, N_Z, stride=N_Y * BITS), :]
+                        for bit in range(BITS)
+                    ],
+                    axis=0,
                 )
-            extra[q, pl.ds(rank, 1), :] = condensed[:, k * PR : (k + 1) * PR]
-            codes = extra[q, CODE_ROW : CODE_ROW + 1, :]
-            codes = jnp.where(row_item == rank, (row_code + slot).astype(jnp.float32), codes)
-            codes = jnp.where(
-                lane == CAP * SHARE + rank, (LOADS + slot).astype(jnp.float32), codes
+                for y in range(N_Y)
+            ]
+
+            which = jnp.where(mine, 0, 1)
+            held = [sums[which, at, rows, :] for at in places]
+            for at, part, before in zip(places, parts, held):
+                sums[which, at, rows, :] = before + part
+            extra[q, pl.ds(slot, 1), :] = (
+                extra[q, pl.ds(slot, 1), :] + condensed[:, k * PR : (k + 1) * PR]
             )
-            extra[q, CODE_ROW : CODE_ROW + 1, :] = codes
         return carry
 
     lax.fori_loop(0, subs, subregion, 0)
-    is_code = iota((8, PR), 0) == CODE_ROW
-    for q in range(plies):
-        rows = extra[q]
-        for y in range(N_Y):
-            turned = rows if y == 0 else pltpu.roll(rows, PR - BITS * y, 1)
-            place = (y * plies + q + LAST) % (N_Y * plies)
-            out_ref[place, CAP * SHARE : CHUNK, :] = jnp.where(
-                is_code, rows, turned
-            ).astype(jnp.bfloat16)
-
-
-def combine_kernel(got_ref, out_ref):
-    plies = got_ref.shape[0] // N_Y
-    sum_rows = iota((LOADS + 8, plies * PR), 0).astype(jnp.float32)
+    twin_ref[:, 0:LOADS, :] = sums[1].astype(jnp.bfloat16)
+    for me in range(CORES):
+
+        @pl.when(core == me)
+        def _():
+            for q in range(plies):
+                rows = extra[q]
+                for y in range(N_Y):
+                    turned = rows if y == 0 else pltpu.roll(rows, PR - BITS * y, 1)
+                    at = (y * (chips // N_Y) + q // CORES - FIRST_CHIP) % chips
+                    if q % CORES == me:
+                        own_loads[at] = turned
+                    else:
+                        twin_ref[at, LOADS:CHUNK, :] = turned.astype(jnp.bfloat16)
+
+
+def merge_kernel(sums, own_loads, other_ref, out_ref):
+    total = sums[0] + other_ref[:, 0:LOADS, :].astype(jnp.float32)
+    out_ref[:, 0:LOADS, :] = total.astype(jnp.bfloat16)
+    loads = own_loads[...] + other_ref[:, LOADS:CHUNK, :].astype(jnp.float32)
+    out_ref[:, LOADS:CHUNK, :] = loads.astype(jnp.bfloat16)
+
+
+def combine_kernel(got_ref, out_ref, totals):
+    chips = got_ref.shape[0]
+    per_y = chips // N_Y
     sums = []
     for y in range(N_Y):
-        messages = [got_ref[(y * plies + q + LAST) % (N_Y * plies)] for q in range(plies)]
-        codes = jnp.concatenate(
-            [
-                m[CAP * SHARE : CHUNK].astype(jnp.float32)[CODE_ROW : CODE_ROW + 1]
-                for m in messages
-            ],
-            axis=1,
-        )
-        choose = (sum_rows == codes).astype(jnp.bfloat16)
-        pad = jnp.zeros((PR - CHUNK, PR), jnp.bfloat16)
-        rows = jnp.concatenate([v for m in messages for v in (m, pad)], axis=0)
-        sums.append(jnp.dot(choose, rows, preferred_element_type=jnp.float32))
+        messages = [got_ref[(y * per_y + x - FIRST_CHIP) % chips] for x in range(per_y)]
+        total = messages[0].astype(jnp.float32)
+        for message in messages[1:]:
+            total = total + message.astype(jnp.float32)
+        totals[y * CHUNK : (y + 1) * CHUNK, :] = total
+        sums.append(total)
     loads = jnp.concatenate([t[LOADS : LOADS + P_OWN] for t in sums], axis=0)
     loads = jnp.concatenate([loads, jnp.zeros((PR - N_Y * P_OWN, PR), jnp.float32)], axis=0)
     loads = loads.T
-    step = BITS * P_OWN
     for z in range(N_Z):
         place = (z - FIRST_Z) % N_Z
-        rows = [t[z * step : (z + 1) * step] for t in sums] + [loads[z * step : z * step + QUAD]]
-        for n, row in enumerate(rows):
-            for half in range(row.shape[0] // QUAD):
-                out_ref[place, n * (step // QUAD) + half] = row[
-                    half * QUAD : (half + 1) * QUAD
-                ].astype(jnp.bfloat16)
+        for y in range(N_Y):
+            for bit in range(BITS):
+                slots = totals[pl.ds(y * CHUNK + bit * N_Z + z, P_OWN, stride=SHARE), :]
+                out_ref[place, y * BITS + bit] = slots.astype(jnp.bfloat16)
+        step = N_Y * BITS
+        out_ref[place, N_Y * BITS] = loads[z * step : z * step + QUAD].astype(jnp.bfloat16)
 
 
 def place_kernel(target_ref, got_ref, blocks_ref, loads_ref, got_blocks, got_loads):
@@ -219,11 +228,16 @@
     touch_slot, interior_inverse, coupling = arguments[1:4]
     subs, inner_size, width = coupling.shape
     plies = lax.axis_size("ply")
+    chips = N_Y * plies // CORES
     return pl.pallas_call(
         condense_kernel,
-        out_shape=jax.ShapeDtypeStruct((N_Y * plies, CHUNK, PR), jnp.bfloat16),
+        out_shape=(
+            jax.ShapeDtypeStruct((CORES, chips, LOADS, PR), jnp.float32),
+            jax.ShapeDtypeStruct((chips, CHUNK - LOADS, PR), jnp.float32),
+            jax.ShapeDtypeStruct((chips, CHUNK, PR), jnp.bfloat16),
+        ),
         in_specs=[pl.BlockSpec(memory_space=pltpu.HBM)] * len(arguments),
-        out_specs=vmem(),
+        out_specs=(vmem(),) * 3,
         scratch_shapes=[
             pltpu.SMEM(touch_slot.shape, jnp.int32),
             pltpu.SMEM(touch_slot.shape, jnp.int32),
@@ -235,7 +249,6 @@
             pltpu.VMEM((24, inner_size), jnp.float32),
             pltpu.VMEM((width, PR), jnp.float32),
             pltpu.VMEM((plies, 8, PR), jnp.float32),
-            pltpu.SMEM((plies,), jnp.int32),
             pltpu.SemaphoreType.DMA((2, subs)),
             pltpu.SemaphoreType.DMA((5,)),
         ],
@@ -244,12 +257,24 @@
     )(*(pltpu.with_memory_space_constraint(argument, pltpu.HBM) for argument in arguments))
 
 
+def merge(sums, own_loads, other):
+    return pl.pallas_call(
+        merge_kernel,
+        out_shape=jax.ShapeDtypeStruct(other.shape, other.dtype),
+        in_specs=[vmem()] * 3,
+        out_specs=vmem(),
+        compiler_params=pltpu.CompilerParams(vmem_limit_bytes=VMEM_LIMIT),
+        name="merge",
+    )(sums, own_loads, other)
+
+
 def combine(got):
     return pl.pallas_call(
         combine_kernel,
         out_shape=jax.ShapeDtypeStruct((N_Z, BACK // QUAD, QUAD, PR), jnp.bfloat16),
         in_specs=[vmem()],
         out_specs=vmem(),
+        scratch_shapes=[pltpu.VMEM((N_Y * CHUNK, PR), jnp.float32)],
         compiler_params=pltpu.CompilerParams(vmem_limit_bytes=VMEM_LIMIT),
         name="combine",
     )(got)
@@ -284,7 +309,7 @@
     touch_slot,
     source_position,
 ):
-    send = condense(
+    sums, own_loads, twin = condense(
         touch_ply.reshape(-1),
         touch_slot,
         interior_inverse,
@@ -293,15 +318,19 @@
         interior_load,
         boundary_load,
     )
-    plane = N_Y * lax.axis_size("ply")
+    plies = lax.axis_size("ply")
+    other = lax.ppermute(twin, "ply", [(q, q ^ 1) for q in range(plies)])
+    chips = N_Y * plies // CORES
     got = lax.all_to_all(
-        send,
+        merge(sums, own_loads, other),
         ("wide", "ply"),
         split_axis=0,
         concat_axis=0,
         tiled=True,
         axis_index_groups=[
-            [z * plane + (i - LAST) % plane for i in range(plane)] for z in range(N_Z)
+            [(z * chips + (i + FIRST_CHIP) % chips) * CORES + core for i in range(chips)]
+            for z in range(N_Z)
+            for core in range(CORES)
         ],
     )
     got = lax.all_to_all(

time: 52.3 us -> 52 us (level)
  blocking collectives: 44.7 us -> 34.2 us
  starting transfers between devices: 0 us -> 8.79 us
  waiting for transfers between devices: 0 us -> 1.56 us
    all_to_all x1, blocking collectives: 23.9 us -> 13.6 us  [on_device(): lax.all_to_all(merge(sums, own_loads, other), ('wide', 'ply'), split_axis...]
    ppermute x0 -> x1, starting transfers between devices: none -> 8.79 us  [on_device(): other = lax.ppermute(twin, 'ply', [(q, q ^ 1) for q in range(plies)])]
    ppermute x0 -> x1, waiting for transfers between devices: none -> 1.56 us  [on_device(): other = lax.ppermute(twin, 'ply', [(q, q ^ 1) for q in range(plies)])]
    pallas_call x1 -> x2, Pallas kernels: 4.85 us -> 5.08 us  [the longest x1 4.99 us: condense(): pl.pallas_call(condense_kernel, out_shape=(jax.ShapeDtypeStruct((CORES, c...]
  transfers between devices with their start and end apart: 0 -> 1, of which waited for: 0 -> 1; matrix products, arithmetic and copies ran while one was open for 0% -> 0% of each run, Pallas kernels for 0% -> 0%
where the time goes in v6:
time: 52 us; the launch traced here: 51.5 us
  blocking collectives  34.2 us (66%)
  starting transfers between devices  8.79 us (17%)
  Pallas kernels  6.35 us (12%)
  waiting for transfers between devices  1.56 us (3%)
  between operations  0.66 us (1%)
    all_to_all x1, blocking collectives, on_device(): lax.all_to_all(combine(got), 'wide', split_axis=0, concat_axis=0, tiled=T...  20.6 us
    all_to_all x1, blocking collectives, on_device(): lax.all_to_all(merge(sums, own_loads, other), ('wide', 'ply'), split_axis...  13.6 us
    ppermute x1, starting transfers between devices, on_device(): other = lax.ppermute(twin, 'ply', [(q, q ^ 1) for q in range(plies)])  8.79 us
    pallas_call x1, Pallas kernels, condense(): pl.pallas_call(condense_kernel, out_shape=(jax.ShapeDtypeStruct((CORES, c...  4.99 us
    ppermute x1, waiting for transfers between devices, on_device(): other = lax.ppermute(twin, 'ply', [(q, q ^ 1) for q in range(plies)])  1.56 us
  transfers between devices with their start and end apart: 1, of which 1 were waited for; matrix products, arithmetic and copies ran while one was open for 0% of the time, Pallas kernels for 0%

profile of v6, /device:TPU:1, one launch (start us, length us, event | category | flops | bytes accessed | tf_op | source)
XLA Modules:
  0.0 51.5 jit_solution(6968303582806885234)
XLA Ops:
  0.6 5.0 %condense.1 = (f32[2,16,128,128]{3,2,1,0:T(8,128)S(1)}, f32[16,8,128]{2,1,0:T(8,128)S(1)}, bf16[16,136,128]{2,1,0:T(8,128)(2,1)S(1)}) custom-call(s32[12]{0:T(128)} %bitcast.1, s32[12]{0:T(128)} %slot_hbm.1, bf16[3,640,640]{2,1,0:T(8,128)(2,1)} %inverse_hbm.1, bf16[3,640,512]{2,1,0:T(8,128)(2,1)} %coupling_hbm.1, bf16[3,512]{1,0:T(4,128)(2,1)} %stiffness_hbm.1, ...), custom_call_target="tpu_custom_call" | custom-call | tf_op jit(solution)/shard_map/condense/pallas_call | solution.py:232
  5.6 8.8 %collective-permute-start = (bf16[16,136,128]{2,1,0:T(8,128)(2,1)S(1)}, bf16[16,136,128]{2,1,0:T(8,128)(2,1)S(1)}, u32[]{:S(2)}, u32[]{:S(2)}) collective-permute-start(bf16[16,136,128]{2,1,0:T(8,128)(2,1)S(1)} %get-tuple-element.7), channel_id=1, source_target_pairs={{0,1},{1,0},{2,3},{3,2},{4,5},{5,4},{6,7},{7,6},{8,9},{9,8},{10,11... | collective-permute-start | bytes 1671176 | tf_op jit(solution)/shard_map/ppermute | solution.py:322
  14.4 1.6 %collective-permute-done.other_ref = bf16[16,136,128]{2,1,0:T(8,128)(2,1)S(1)} collective-permute-done((bf16[16,136,128]{2,1,0:T(8,128)(2,1)S(1)}, bf16[16,136,128]{2,1,0:T(8,128)(2,1)S(1)}, u32[]{:S(2)}, u32[]{:S(2)}) %collective-permute-start) | collective-permute-done | bytes 557088 | tf_op jit(solution)/shard_map/ppermute | solution.py:322
  16.0 0.0 copy-start
  16.0 0.1 merge.1
  16.1 13.6 %all_to_all.10.got_ref = bf16[16,136,128]{2,1,0:T(8,128)(2,1)S(1)} all-to-all(bf16[16,136,128]{2,1,0:T(8,128)(2,1)S(1)} %merge.1), channel_id=1, replica_groups={{20,22,24,26,28,30,0,2,4,6,8,10,12,14,16,18},{21,23,25,27,29,31,1,3,5,7..., dimensions={0} | all-to-all | bytes 1114112 | tf_op jit(solution)/shard_map/all_to_all | solution.py:324
  29.7 0.2 combine.1
  30.0 20.6 %all_to_all.11.got_ref = bf16[16,9,4,128]{3,2,1,0:T(4,128)(2,1)S(1)} all-to-all(bf16[16,9,4,128]{3,2,1,0:T(4,128)(2,1)S(1)} %combine.1), channel_id=1, replica_groups={{320,352,384,416,448,480,0,32,64,96,128,160,192,224,256,288},{328,360,3..., dimensions={0} | all-to-all | bytes 294912 | tf_op jit(solution)/shard_map/all_to_all | solution.py:336
  50.5 0.0 copy-done
  50.5 1.0 %place.1 = (f32[1,2,256,128]{3,2,1,0:T(8,128)}, f32[1,2,256]{2,1,0:T(2,128)}) custom-call(s32[1,256]{1,0:T(1,128)S(1)} %copy-done, bf16[16,9,4,128]{3,2,1,0:T(4,128)(2,1)S(1)} %all_to_all.11.got_ref), custom_call_target="tpu_custom_call" | custom-call | tf_op jit(solution)/shard_map/place/pallas_call | solution.py:285
Async XLA Ops:
  5.6 10.4 %collective-permute-start = (bf16[16,136,128]{2,1,0:T(8,128)(2,1)S(1)}, bf16[16,136,128]{2,1,0:T(8,128)(2,1)S(1)}, u32[]{:S(2)}, u32[]{:S(2)}) collective-permute-start(bf16[16,136,128]{2,1,0:T(8,128)(2,1)S(1)} %get-tuple-element.7), channel_id=1, source_target_pairs={{0,1},{1,0},{2,3},{3,2},{4,5},{5,4},{6,7},{7,6},{8,9},{9,8},{10,11... | collective-permute-start | bytes 1671176 | tf_op jit(solution)/shard_map/ppermute | solution.py:322
  16.0 34.5 %copy-start = (s32[1,256]{1,0:T(1,128)S(1)}, s32[1,256]{1,0:T(1,128)}, u32[]{:S(2)}) copy-start(s32[1,256]{1,0:T(1,128)} %target_ref.1) | copy-start | bytes 3076

commit v7 on v5

--- a/solution.py
+++ b/solution.py
@@ -18,8 +18,11 @@
 LOADS = SHARE * P_OWN
 QUAD = 4
 BACK = N_Y * P_OWN * BITS + QUAD
-FIRST_Z = 10
-LAST = 11
+Z_ORDER = (11, 6, 8, 15, 12, 3, 10, 5, 2, 14, 0, 4, 7, 1, 9, 13)
+PLANE_ORDER = (
+    21, 9, 24, 14, 10, 28, 1, 5, 3, 22, 23, 13, 12, 29, 16, 27,
+    6, 31, 8, 25, 0, 26, 2, 30, 20, 15, 19, 11, 4, 17, 18, 7,
+)
 VMEM_LIMIT = 40 * 1024 * 1024
 
 
@@ -47,6 +50,7 @@
     panels,
     extra,
     count,
+    places,
     sems,
     small_sems,
 ):
@@ -76,6 +80,8 @@
     extra[...] = jnp.where(iota(extra.shape, 1) == CODE_ROW, -1.0, 0.0)
     for q in range(plies):
         count[q] = 0
+    for place, device in enumerate(PLANE_ORDER):
+        places[device] = place
     lane = iota((1, PR), 1)
     row_code = (lane % N_Z) * (BITS * P_OWN) + ((lane // N_Z) % BITS) * P_OWN
     row_item = lane // SHARE
@@ -86,12 +92,11 @@
     rows_ref[8 : 8 + subs, 0:inner_size] = interior_ref[...].astype(jnp.float32)
     rows_ref[16 : 16 + subs, 0:width] = boundary_ref[...].astype(jnp.float32)
 
-    def subregion(s, carry):
+    def subregion(s):
         for copy in sub_copies(s):
             copy.wait()
 
-        @pl.when(s + 2 < subs)
-        def _():
+        if s + 2 < subs:
             for copy in sub_copies(s + 2):
                 copy.start()
 
@@ -112,7 +117,7 @@
             product = jnp.dot(
                 turned[columns], inner[:, columns], preferred_element_type=jnp.float32
             )
-            panels[columns, :] = jnp.where(same, stiffness[:, columns], 0.0) - product
+            panels[s, columns, :] = jnp.where(same, stiffness[:, columns], 0.0) - product
         for k in range(NPS):
             item = s * NPS + k
             q = ply_ref[item]
@@ -121,10 +126,10 @@
             count[q] = rank + 1
             for y in range(N_Y):
                 part = [
-                    panels[pl.ds(k * PR + y * BITS + bit, N_Z, stride=N_Y * BITS), :]
+                    panels[s, pl.ds(k * PR + y * BITS + bit, N_Z, stride=N_Y * BITS), :]
                     for bit in range(BITS)
                 ]
-                place = lax.rem(y * plies + q + LAST, N_Y * plies)
+                place = places[y * plies + q]
                 out_ref[place, pl.ds(pl.multiple_of(rank * SHARE, SHARE), SHARE), :] = (
                     jnp.concatenate(part, axis=0).astype(jnp.bfloat16)
                 )
@@ -135,15 +140,14 @@
                 lane == CAP * SHARE + rank, (LOADS + slot).astype(jnp.float32), codes
             )
             extra[q, CODE_ROW : CODE_ROW + 1, :] = codes
-        return carry
-
-    lax.fori_loop(0, subs, subregion, 0)
+    for s in range(subs):
+        subregion(s)
     is_code = iota((8, PR), 0) == CODE_ROW
     for q in range(plies):
         rows = extra[q]
         for y in range(N_Y):
             turned = rows if y == 0 else pltpu.roll(rows, PR - BITS * y, 1)
-            place = (y * plies + q + LAST) % (N_Y * plies)
+            place = PLANE_ORDER.index(y * plies + q)
             out_ref[place, CAP * SHARE : CHUNK, :] = jnp.where(
                 is_code, rows, turned
             ).astype(jnp.bfloat16)
@@ -154,7 +158,7 @@
     sum_rows = iota((LOADS + 8, plies * PR), 0).astype(jnp.float32)
     sums = []
     for y in range(N_Y):
-        messages = [got_ref[(y * plies + q + LAST) % (N_Y * plies)] for q in range(plies)]
+        messages = [got_ref[PLANE_ORDER.index(y * plies + q)] for q in range(plies)]
         codes = jnp.concatenate(
             [
                 m[CAP * SHARE : CHUNK].astype(jnp.float32)[CODE_ROW : CODE_ROW + 1]
@@ -171,7 +175,7 @@
     loads = loads.T
     step = BITS * P_OWN
     for z in range(N_Z):
-        place = (z - FIRST_Z) % N_Z
+        place = Z_ORDER.index(z)
         rows = [t[z * step : (z + 1) * step] for t in sums] + [loads[z * step : z * step + QUAD]]
         for n, row in enumerate(rows):
             for half in range(row.shape[0] // QUAD):
@@ -183,7 +187,11 @@
 def place_kernel(target_ref, got_ref, blocks_ref, loads_ref, got_blocks, got_loads):
     patches = target_ref.shape[1]
     z_owners = N_Y * P_OWN
-    target = lax.rem(target_ref[...] + (N_Z - FIRST_Z) * z_owners, N_Z * z_owners)
+    target = target_ref[...]
+    first = jnp.zeros_like(target)
+    for place, z in enumerate(Z_ORDER):
+        first = jnp.where(target // z_owners == z, place * z_owners, first)
+    target = first + target % z_owners
     rows = N_Y * P_OWN * BITS
     got_loads[...] = jnp.zeros_like(got_loads)
     for z in range(N_Z):
@@ -233,9 +241,10 @@
             pltpu.VMEM((subs, inner_size), jnp.bfloat16),
             pltpu.VMEM((subs, width), jnp.bfloat16),
             pltpu.VMEM((24, inner_size), jnp.float32),
-            pltpu.VMEM((width, PR), jnp.float32),
+            pltpu.VMEM((subs, width, PR), jnp.float32),
             pltpu.VMEM((plies, 8, PR), jnp.float32),
             pltpu.SMEM((plies,), jnp.int32),
+            pltpu.SMEM((N_Y * plies,), jnp.int32),
             pltpu.SemaphoreType.DMA((2, subs)),
             pltpu.SemaphoreType.DMA((5,)),
         ],
@@ -300,9 +309,7 @@
         split_axis=0,
         concat_axis=0,
         tiled=True,
-        axis_index_groups=[
-            [z * plane + (i - LAST) % plane for i in range(plane)] for z in range(N_Z)
-        ],
+        axis_index_groups=[[z * plane + i for i in PLANE_ORDER] for z in range(N_Z)],
     )
     got = lax.all_to_all(
         combine(got),
@@ -310,9 +317,7 @@
         split_axis=0,
         concat_axis=0,
         tiled=True,
-        axis_index_groups=[
-            [(i + FIRST_Z) % N_Z * N_Y + y for i in range(N_Z)] for y in range(N_Y)
-        ],
+        axis_index_groups=[[z * N_Y + y for z in Z_ORDER] for y in range(N_Y)],
     )
     return place(source_position, got)
 

time: 52.3 us -> 51.6 us (0.987)
  blocking collectives: 44.7 us -> 43.7 us
    all_to_all x1, blocking collectives: 20.8 us -> 20 us  [on_device(): lax.all_to_all(combine(got), 'wide', split_axis=0, concat_axis=0, tiled=T...]
where the time goes in v7:
time: 51.6 us; the launch traced here: 50.7 us
  blocking collectives  43.7 us (85%)
  Pallas kernels  6.26 us (12%)
  between operations  0.65 us (1%)
    all_to_all x1, blocking collectives, on_device(): lax.all_to_all(send, ('wide', 'ply'), split_axis=0, concat_axis=0, tiled=...  23.7 us
    all_to_all x1, blocking collectives, on_device(): lax.all_to_all(combine(got), 'wide', split_axis=0, concat_axis=0, tiled=T...  20 us
    pallas_call x1, Pallas kernels, condense(): pl.pallas_call(condense_kernel, out_shape=jax.ShapeDtypeStruct((N_Y * pli...  4.69 us

profile of v7, /device:TPU:1, one launch (start us, length us, event | category | flops | bytes accessed | tf_op | source)
XLA Modules:
  0.0 50.7 jit_solution(3408099439220227238)
XLA Ops:
  0.6 4.7 %condense.1 = bf16[32,104,128]{2,1,0:T(8,128)(2,1)S(1)} custom-call(s32[12]{0:T(128)} %bitcast.1, s32[12]{0:T(128)} %slot_hbm.1, bf16[3,640,640]{2,1,0:T(8,128)(2,1)} %inverse_hbm.1, bf16[3,640,512]{2,1,0:T(8,128)(2,1)} %coupling_hbm.1, bf16[3,512]{1,0:T(4,128)(2,1)} %stiffness_hbm.1, bf16[3,640]{1,0:T(4,128)(2,1)} %interior_hbm.1, bf16[3,512]{1,0:T(4,128)(2,1)} %boundary_hbm.1), custom_call_target="tpu_custom_call" | custom-call | tf_op jit(solution)/shard_map/condense/pallas_call | solution.py:230
  5.3 0.0 copy-start
  5.3 23.7 %all_to_all.10.got_ref = bf16[32,104,128]{2,1,0:T(8,128)(2,1)S(1)} all-to-all(bf16[32,104,128]{2,1,0:T(8,128)(2,1)S(1)} %condense.1), channel_id=1, replica_groups={{21,9,24,14,10,28,1,5,3,22,23,13,12,29,16,27,6,31,8,25,0,26,2,30,20,15,..., dimensions={0} | all-to-all | bytes 1703936 | tf_op jit(solution)/shard_map/all_to_all | solution.py:306
  29.1 0.6 %combine.1 = bf16[16,9,4,128]{3,2,1,0:T(4,128)(2,1)S(1)} custom-call(bf16[32,104,128]{2,1,0:T(8,128)(2,1)S(1)} %all_to_all.10.got_ref), custom_call_target="tpu_custom_call" | custom-call | tf_op jit(solution)/shard_map/combine/pallas_call | solution.py:257
  29.6 20.0 %all_to_all.11.got_ref = bf16[16,9,4,128]{3,2,1,0:T(4,128)(2,1)S(1)} all-to-all(bf16[16,9,4,128]{3,2,1,0:T(4,128)(2,1)S(1)} %combine.1), channel_id=1, replica_groups={{352,192,256,480,384,96,320,160,64,448,0,128,224,32,288,416},{360,200,2..., dimensions={0} | all-to-all | bytes 294912 | tf_op jit(solution)/shard_map/all_to_all | solution.py:314
  49.6 0.0 copy-done
  49.6 1.0 %place.1 = (f32[1,2,256,128]{3,2,1,0:T(8,128)}, f32[1,2,256]{2,1,0:T(2,128)}) custom-call(s32[1,256]{1,0:T(1,128)S(1)} %copy-done, bf16[16,9,4,128]{3,2,1,0:T(4,128)(2,1)S(1)} %all_to_all.11.got_ref), custom_call_target="tpu_custom_call" | custom-call | tf_op jit(solution)/shard_map/place/pallas_call | solution.py:269
Async XLA Ops:
  5.3 44.3 %copy-start = (s32[1,256]{1,0:T(1,128)S(1)}, s32[1,256]{1,0:T(1,128)}, u32[]{:S(2)}) copy-start(s32[1,256]{1,0:T(1,128)} %target_ref.1) | copy-start | bytes 3076

commit v8 on v6

--- a/solution.py
+++ b/solution.py
@@ -17,8 +17,8 @@
 CHUNK = LOADS + 8
 QUAD = 4
 BACK = N_Y * P_OWN * BITS + QUAD
-FIRST_Z = 10
-FIRST_CHIP = 10
+Z_ORDER = (11, 6, 8, 15, 12, 3, 10, 5, 2, 14, 0, 4, 7, 1, 9, 13)
+CHIP_ORDER = (10, 3, 13, 15, 7, 12, 4, 14, 9, 8, 1, 0, 11, 6, 2, 5)
 VMEM_LIMIT = 40 * 1024 * 1024
 
 
@@ -47,6 +47,7 @@
     rows_ref,
     panels,
     extra,
+    table,
     sems,
     small_sems,
 ):
@@ -76,6 +77,8 @@
         copy.start()
     sums[...] = jnp.zeros_like(sums)
     extra[...] = jnp.zeros_like(extra)
+    for place, chip in enumerate(CHIP_ORDER):
+        table[chip] = place
     same = iota((PR, PR), 0) == iota((PR, PR), 1)
     for copy in small:
         copy.wait()
@@ -83,12 +86,11 @@
     rows_ref[8 : 8 + subs, 0:inner_size] = interior_ref[...].astype(jnp.float32)
     rows_ref[16 : 16 + subs, 0:width] = boundary_ref[...].astype(jnp.float32)
 
-    def subregion(s, carry):
+    def subregion(s):
         for copy in sub_copies(s):
             copy.wait()
 
-        @pl.when(s + 2 < subs)
-        def _():
+        if s + 2 < subs:
             for copy in sub_copies(s + 2):
                 copy.start()
 
@@ -109,7 +111,7 @@
             product = jnp.dot(
                 turned[columns], inner[:, columns], preferred_element_type=jnp.float32
             )
-            panels[columns, :] = jnp.where(same, stiffness[:, columns], 0.0) - product
+            panels[s, columns, :] = jnp.where(same, stiffness[:, columns], 0.0) - product
         for k in range(NPS):
             item = s * NPS + k
             q = ply_ref[item]
@@ -118,13 +120,13 @@
 
             rows = pl.ds(pl.multiple_of(slot * SHARE, SHARE), SHARE)
             places = [
-                lax.rem(y * (chips // N_Y) + q // CORES + chips - FIRST_CHIP, chips)
+                table[y * (chips // N_Y) + q // CORES]
                 for y in range(N_Y)
             ]
             parts = [
                 jnp.concatenate(
                     [
-                        panels[pl.ds(k * PR + y * BITS + bit, N_Z, stride=N_Y * BITS), :]
+                        panels[s, pl.ds(k * PR + y * BITS + bit, N_Z, stride=N_Y * BITS), :]
                         for bit in range(BITS)
                     ],
                     axis=0,
@@ -139,9 +141,8 @@
             extra[q, pl.ds(slot, 1), :] = (
                 extra[q, pl.ds(slot, 1), :] + condensed[:, k * PR : (k + 1) * PR]
             )
-        return carry
-
-    lax.fori_loop(0, subs, subregion, 0)
+    for s in range(subs):
+        subregion(s)
     twin_ref[:, 0:LOADS, :] = sums[1].astype(jnp.bfloat16)
     for me in range(CORES):
 
@@ -151,7 +152,7 @@
                 rows = extra[q]
                 for y in range(N_Y):
                     turned = rows if y == 0 else pltpu.roll(rows, PR - BITS * y, 1)
-                    at = (y * (chips // N_Y) + q // CORES - FIRST_CHIP) % chips
+                    at = CHIP_ORDER.index(y * (chips // N_Y) + q // CORES)
                     if q % CORES == me:
                         own_loads[at] = turned
                     else:
@@ -170,7 +171,7 @@
     per_y = chips // N_Y
     sums = []
     for y in range(N_Y):
-        messages = [got_ref[(y * per_y + x - FIRST_CHIP) % chips] for x in range(per_y)]
+        messages = [got_ref[CHIP_ORDER.index(y * per_y + x)] for x in range(per_y)]
         total = messages[0].astype(jnp.float32)
         for message in messages[1:]:
             total = total + message.astype(jnp.float32)
@@ -180,7 +181,7 @@
     loads = jnp.concatenate([loads, jnp.zeros((PR - N_Y * P_OWN, PR), jnp.float32)], axis=0)
     loads = loads.T
     for z in range(N_Z):
-        place = (z - FIRST_Z) % N_Z
+        place = Z_ORDER.index(z)
         for y in range(N_Y):
             for bit in range(BITS):
                 slots = totals[pl.ds(y * CHUNK + bit * N_Z + z, P_OWN, stride=SHARE), :]
@@ -192,7 +193,11 @@
 def place_kernel(target_ref, got_ref, blocks_ref, loads_ref, got_blocks, got_loads):
     patches = target_ref.shape[1]
     z_owners = N_Y * P_OWN
-    target = lax.rem(target_ref[...] + (N_Z - FIRST_Z) * z_owners, N_Z * z_owners)
+    target = target_ref[...]
+    first = jnp.zeros_like(target)
+    for place, z in enumerate(Z_ORDER):
+        first = jnp.where(target // z_owners == z, place * z_owners, first)
+    target = first + target % z_owners
     rows = N_Y * P_OWN * BITS
     got_loads[...] = jnp.zeros_like(got_loads)
     for z in range(N_Z):
@@ -247,8 +252,9 @@
             pltpu.VMEM((subs, inner_size), jnp.bfloat16),
             pltpu.VMEM((subs, width), jnp.bfloat16),
             pltpu.VMEM((24, inner_size), jnp.float32),
-            pltpu.VMEM((width, PR), jnp.float32),
+            pltpu.VMEM((subs, width, PR), jnp.float32),
             pltpu.VMEM((plies, 8, PR), jnp.float32),
+            pltpu.SMEM((chips,), jnp.int32),
             pltpu.SemaphoreType.DMA((2, subs)),
             pltpu.SemaphoreType.DMA((5,)),
         ],
@@ -328,7 +334,7 @@
         concat_axis=0,
         tiled=True,
         axis_index_groups=[
-            [(z * chips + (i + FIRST_CHIP) % chips) * CORES + core for i in range(chips)]
+            [(z * chips + chip) * CORES + core for chip in CHIP_ORDER]
             for z in range(N_Z)
             for core in range(CORES)
         ],
@@ -339,9 +345,7 @@
         split_axis=0,
         concat_axis=0,
         tiled=True,
-        axis_index_groups=[
-            [(i + FIRST_Z) % N_Z * N_Y + y for i in range(N_Z)] for y in range(N_Y)
-        ],
+        axis_index_groups=[[z * N_Y + y for z in Z_ORDER] for y in range(N_Y)],
     )
     return place(source_position, got)
 

time: 52 us -> 51.3 us (0.987)
  the two profiles are of different devices: /device:TPU:1 before, /device:TPU:2 now
where the time goes in v8:
time: 51.3 us; the launch traced here: 51.1 us
  blocking collectives  40.2 us (78%)
  Pallas kernels  6.34 us (12%)
  starting transfers between devices  1.92 us (4%)
  waiting for transfers between devices  1.92 us (4%)
  between operations  0.66 us (1%)
    all_to_all x1, blocking collectives, on_device(): lax.all_to_all(combine(got), 'wide', split_axis=0, concat_axis=0, tiled=T...  20.7 us
    all_to_all x1, blocking collectives, on_device(): lax.all_to_all(merge(sums, own_loads, other), ('wide', 'ply'), split_axis...  19.5 us
    pallas_call x1, Pallas kernels, condense(): pl.pallas_call(condense_kernel, out_shape=(jax.ShapeDtypeStruct((CORES, c...  5 us
    ppermute x1, waiting for transfers between devices, on_device(): other = lax.ppermute(twin, 'ply', [(q, q ^ 1) for q in range(plies)])  1.92 us
    ppermute x1, starting transfers between devices, on_device(): other = lax.ppermute(twin, 'ply', [(q, q ^ 1) for q in range(plies)])  1.92 us
  transfers between devices with their start and end apart: 1, of which 1 were waited for; matrix products, arithmetic and copies ran while one was open for 0% of the time, Pallas kernels for 0%

profile of v8, /device:TPU:2, one launch (start us, length us, event | category | flops | bytes accessed | tf_op | source)
XLA Modules:
  0.0 51.1 jit_solution(17472866791818549889)
XLA Ops:
  0.6 5.0 %condense.1 = (f32[2,16,128,128]{3,2,1,0:T(8,128)S(1)}, f32[16,8,128]{2,1,0:T(8,128)S(1)}, bf16[16,136,128]{2,1,0:T(8,128)(2,1)S(1)}) custom-call(s32[12]{0:T(128)} %bitcast.1, s32[12]{0:T(128)} %slot_hbm.1, bf16[3,640,640]{2,1,0:T(8,128)(2,1)} %inverse_hbm.1, bf16[3,640,512]{2,1,0:T(8,128)(2,1)} %coupling_hbm.1, bf16[3,512]{1,0:T(4,128)(2,1)} %stiffness_hbm.1, ...), custom_call_target="tpu_custom_call" | custom-call | tf_op jit(solution)/shard_map/condense/pallas_call | solution.py:237
  5.6 1.9 %collective-permute-start = (bf16[16,136,128]{2,1,0:T(8,128)(2,1)S(1)}, bf16[16,136,128]{2,1,0:T(8,128)(2,1)S(1)}, u32[]{:S(2)}, u32[]{:S(2)}) collective-permute-start(bf16[16,136,128]{2,1,0:T(8,128)(2,1)S(1)} %get-tuple-element.7), channel_id=1, source_target_pairs={{0,1},{1,0},{2,3},{3,2},{4,5},{5,4},{6,7},{7,6},{8,9},{9,8},{10,11... | collective-permute-start | bytes 1671176 | tf_op jit(solution)/shard_map/ppermute | solution.py:328
  7.6 1.9 %collective-permute-done.other_ref = bf16[16,136,128]{2,1,0:T(8,128)(2,1)S(1)} collective-permute-done((bf16[16,136,128]{2,1,0:T(8,128)(2,1)S(1)}, bf16[16,136,128]{2,1,0:T(8,128)(2,1)S(1)}, u32[]{:S(2)}, u32[]{:S(2)}) %collective-permute-start) | collective-permute-done | bytes 557088 | tf_op jit(solution)/shard_map/ppermute | solution.py:328
  9.5 0.0 copy-start
  9.5 0.1 merge.1
  9.6 19.5 %all_to_all.10.got_ref = bf16[16,136,128]{2,1,0:T(8,128)(2,1)S(1)} all-to-all(bf16[16,136,128]{2,1,0:T(8,128)(2,1)S(1)} %merge.1), channel_id=1, replica_groups={{20,6,26,30,14,24,8,28,18,16,2,0,22,12,4,10},{21,7,27,31,15,25,9,29,19,..., dimensions={0} | all-to-all | bytes 1114112 | tf_op jit(solution)/shard_map/all_to_all | solution.py:330
  29.1 0.2 combine.1
  29.3 20.7 %all_to_all.11.got_ref = bf16[16,9,4,128]{3,2,1,0:T(4,128)(2,1)S(1)} all-to-all(bf16[16,9,4,128]{3,2,1,0:T(4,128)(2,1)S(1)} %combine.1), channel_id=1, replica_groups={{352,192,256,480,384,96,320,160,64,448,0,128,224,32,288,416},{360,200,2..., dimensions={0} | all-to-all | bytes 294912 | tf_op jit(solution)/shard_map/all_to_all | solution.py:342
  50.1 0.0 copy-done
  50.1 1.0 %place.1 = (f32[1,2,256,128]{3,2,1,0:T(8,128)}, f32[1,2,256]{2,1,0:T(2,128)}) custom-call(s32[1,256]{1,0:T(1,128)S(1)} %copy-done, bf16[16,9,4,128]{3,2,1,0:T(4,128)(2,1)S(1)} %all_to_all.11.got_ref), custom_call_target="tpu_custom_call" | custom-call | tf_op jit(solution)/shard_map/place/pallas_call | solution.py:291
Async XLA Ops:
  5.6 3.9 %collective-permute-start = (bf16[16,136,128]{2,1,0:T(8,128)(2,1)S(1)}, bf16[16,136,128]{2,1,0:T(8,128)(2,1)S(1)}, u32[]{:S(2)}, u32[]{:S(2)}) collective-permute-start(bf16[16,136,128]{2,1,0:T(8,128)(2,1)S(1)} %get-tuple-element.7), channel_id=1, source_target_pairs={{0,1},{1,0},{2,3},{3,2},{4,5},{5,4},{6,7},{7,6},{8,9},{9,8},{10,11... | collective-permute-start | bytes 1671176 | tf_op jit(solution)/shard_map/ppermute | solution.py:328
  9.5 40.6 %copy-start = (s32[1,256]{1,0:T(1,128)S(1)}, s32[1,256]{1,0:T(1,128)}, u32[]{:S(2)}) copy-start(s32[1,256]{1,0:T(1,128)} %target_ref.1) | copy-start | bytes 3076
